TPU v7x, 128 devices: a whole 4x4x4 slice. The times are simulated.
128 devices in a mesh: rows: 16 (over y, x), cols: 8 (over z, core).
Axes of the slice: x: 4, y: 4, z: 4, core: 2. Of those that a mesh axis runs over, the one named last changes fastest.
Arguments:
- matrix: float32 [32768, 1024], P('rows', 'cols'), may hold values from -48 to 48
- partners: int32 [2, 8], replicated, may hold values from 0 to 7, each once within a row
Outputs:
- rotated: float32 [32768, 1024], P('rows', 'cols')
Inputs may be any that keep to these rules, and one draw needn't show every extreme that they name: Each row of partners names every block once.
All inputs are finite; a program needn't handle non-finite values.
Results may differ from a plain program's by a relative error of at most 0.00028.
Values sent between devices are 32-bit elements; how exact they have to be, the bound alone decides.
A program may use at most 64 MiB of HBM per device.

v0:
```python
import jax
import jax.numpy as jnp
from jax import lax
from jax.sharding import PartitionSpec as P

CYCLE = 3
MATCHED = 2
STEPS = 12


epsilon = 1e-06
highest = lax.Precision.HIGHEST


def from_behind(array, axis, by):
    count = lax.axis_size(axis)
    return lax.ppermute(array, axis, [(i, (i + by) % count) for i in range(count)])


def start_iterate(gram_full):
    order = gram_full.shape[0]
    scale = lax.rsqrt(jnp.diagonal(gram_full) + epsilon)
    normed = gram_full * scale[:, None] * scale[None, :]
    kernel = jnp.eye(order, dtype=jnp.float32) + jnp.triu(normed, 1) - jnp.tril(normed, -1)
    return kernel / jnp.sqrt(jnp.sum(kernel * kernel))


def polar_whole(start):

    def advance(counter, current):
        inner = jnp.dot(current.T, current, precision=highest)
        return 1.5 * current - 0.5 * jnp.dot(current, inner, precision=highest)

    return lax.fori_loop(0, STEPS, advance, start)


def body(matrix, partners):
    current = matrix
    row_count, width = current.shape
    groups = lax.axis_size("cols")
    for meeting in range(CYCLE + MATCHED):
        if meeting < CYCLE:
            other = from_behind(current, "cols", meeting + 1)
        else:
            pieces = current.reshape(groups, row_count // groups, width)
            spread = lax.all_to_all(pieces, "cols", split_axis=0, concat_axis=0, tiled=True)
            chosen = jnp.take(spread, partners[meeting - CYCLE], axis=0)
            other = lax.all_to_all(chosen, "cols", split_axis=0, concat_axis=0, tiled=True).reshape(
                row_count, width
            )
        paired = jnp.concatenate([other, current], axis=1)
        local_gram = jnp.einsum("ra,rb->ab", paired, paired, precision=highest)
        gram_sum = lax.psum(local_gram, "rows")
        start = start_iterate(gram_sum)
        rotation = polar_whole(start)
        current = jnp.dot(paired, rotation[:, width:], precision=highest)
    return current


def solution(mesh):
    placed = (P("rows", "cols"), P())
    return jax.shard_map(
        body, mesh=mesh, in_specs=placed, out_specs=P("rows", "cols"), check_vma=False
    )
```

profile of v0, /device:TPU:1, one launch (start us, length us, event | category | flops | bytes accessed | tf_op | source)
XLA Modules:
  0.0 704.4 jit_solution(10862355111871873727)
XLA Ops:
  9.6 12.1 %collective-permute-done = f32[2048,128]{1,0:T(8,128)S(1)} collective-permute-done((f32[2048,128]{1,0:T(8,128)}, f32[2048,128]{1,0:T(8,128)S(1)}, u32[]{:S(2)}, u32[]{:S(2)}) %collective-permute-start) | collective-permute-done | bytes 1048608 | tf_op jit(solution)/shard_map/ppermute | solution.py:17
  21.8 4.3 fusion.42
  26.2 85.4 %all-reduce.6.cloned.1.call-done = f32[256,256]{1,0:T(8,128)} async-done(((f32[256,256]{1,0:T(8,128)}), f32[256,256]{1,0:T(8,128)}) %all-reduce.6.cloned.1.call-update) | async-done | bytes 262160 | tf_op jit(solution)/shard_map/psum | solution.py:53
  117.8 12.8 %while.50 = (s32[]{:T(128)}, f32[256,256]{0,1:T(8,128)S(1)}, s32[]{:T(128)}) while((s32[]{:T(128)}, f32[256,256]{0,1:T(8,128)S(1)}, s32[]{:T(128)}) %tuple.85), condition=%wide.region_3.4_spmd, body=%wide.region_2.3_spmd.sunk | while | flops 402849792 | bytes 1835053 | solution.py:34
  134.2 22.7 %collective-permute-done.1 = f32[2048,128]{0,1:T(8,128)S(1)} collective-permute-done((f32[2048,128]{0,1:T(8,128)S(1)}, f32[2048,128]{0,1:T(8,128)S(1)}, u32[]{:S(2)}, u32[]{:S(2)}) %collective-permute-start.1) | collective-permute-done | bytes 1048608 | tf_op jit(solution)/shard_map/ppermute | solution.py:17
  160.0 82.2 %all-reduce.8.cloned.1.call-done = f32[256,256]{1,0:T(8,128)} async-done(((f32[256,256]{1,0:T(8,128)}), f32[256,256]{1,0:T(8,128)}) %all-reduce.8.cloned.1.call-update) | async-done | bytes 262160 | tf_op jit(solution)/shard_map/psum | solution.py:53
  248.5 12.8 %while.51 = (s32[]{:T(128)}, f32[256,256]{0,1:T(8,128)S(1)}, s32[]{:T(128)}) while((s32[]{:T(128)}, f32[256,256]{0,1:T(8,128)S(1)}, s32[]{:T(128)}) %tuple.88), condition=%wide.region_7.8_spmd, body=%wide.region_6.7_spmd.sunk | while | flops 402849792 | bytes 1835053 | solution.py:34
  262.6 4.8 collective-permute-start.2
  267.3 23.6 %collective-permute-done.2 = f32[2048,128]{0,1:T(8,128)S(1)} collective-permute-done((f32[2048,128]{0,1:T(8,128)S(1)}, f32[2048,128]{0,1:T(8,128)S(1)}, u32[]{:S(2)}, u32[]{:S(2)}) %collective-permute-start.2) | collective-permute-done | bytes 1048608 | tf_op jit(solution)/shard_map/ppermute | solution.py:17
  293.5 79.8 %all-reduce.10.cloned.1.call-done = f32[256,256]{1,0:T(8,128)} async-done(((f32[256,256]{1,0:T(8,128)}), f32[256,256]{1,0:T(8,128)}) %all-reduce.10.cloned.1.call-update) | async-done | bytes 262160 | tf_op jit(solution)/shard_map/psum | solution.py:53
  379.6 12.8 %while.52 = (s32[]{:T(128)}, f32[256,256]{0,1:T(8,128)S(1)}, s32[]{:T(128)}) while((s32[]{:T(128)}, f32[256,256]{0,1:T(8,128)S(1)}, s32[]{:T(128)}) %tuple.91), condition=%wide.region_11.12_spmd, body=%wide.region_10.11_spmd.sunk | while | flops 402849792 | bytes 1835053 | solution.py:34
  392.3 4.5 fusion.14
  396.9 6.4 all-to-all-start
  403.3 15.1 %all-to-all-done = f32[8,256,128]{2,1,0:T(8,128)S(1)} async-done(((f32[8,256,128]{2,1,0:T(8,128)}), f32[8,256,128]{2,1,0:T(8,128)S(1)}, u32[]{:S(2)}, u32[]{:S(2)}) %all-to-all-start) | async-done | bytes 1048608 | tf_op jit(solution)/shard_map/all_to_all | solution.py:46
  419.1 18.5 %all_to_all.20 = f32[8,256,128]{2,1,0:T(8,128)S(1)} all-to-all(f32[8,256,128]{2,1,0:T(8,128)S(1)} %broadcast_select_fusion.1), channel_id=1, replica_groups=mesh['rows'=16,'cols'=8] {'cols'}, dimensions={0} | all-to-all | bytes 2097152 | tf_op jit(solution)/shard_map/all_to_all | solution.py:48
  437.6 5.8 fusion.13
  443.5 80.7 %all-reduce.12.cloned.1.call-done = f32[256,256]{1,0:T(8,128)} async-done(((f32[256,256]{1,0:T(8,128)}), f32[256,256]{1,0:T(8,128)}) %all-reduce.12.cloned.1.call-update) | async-done | bytes 262160 | tf_op jit(solution)/shard_map/psum | solution.py:53
  530.4 12.7 %while.53 = (s32[]{:T(128)}, f32[256,256]{0,1:T(8,128)S(1)}, s32[]{:T(128)}) while((s32[]{:T(128)}, f32[256,256]{0,1:T(8,128)S(1)}, s32[]{:T(128)}) %tuple.94), condition=%wide.region_15.17_spmd, body=%wide.region_14.16_spmd.sunk | while | flops 402849792 | bytes 1835053 | solution.py:34
  547.2 6.4 all-to-all-start.2
  553.6 15.1 %all-to-all-done.2 = f32[8,256,128]{2,1,0:T(8,128)S(1)} async-done(((f32[8,256,128]{2,1,0:T(8,128)}), f32[8,256,128]{2,1,0:T(8,128)S(1)}, u32[]{:S(2)}, u32[]{:S(2)}) %all-to-all-start.2) | async-done | bytes 1048608 | tf_op jit(solution)/shard_map/all_to_all | solution.py:46
  569.4 18.6 %all_to_all.21 = f32[8,256,128]{2,1,0:T(8,128)S(1)} all-to-all(f32[8,256,128]{2,1,0:T(8,128)S(1)} %broadcast_select_fusion), channel_id=1, replica_groups=mesh['rows'=16,'cols'=8] {'cols'}, dimensions={0} | all-to-all | bytes 2097152 | tf_op jit(solution)/shard_map/all_to_all | solution.py:48
  588.0 5.9 fusion.11
  593.9 80.7 %all-reduce.14.cloned.1.call-done = f32[256,256]{1,0:T(8,128)} async-done(((f32[256,256]{1,0:T(8,128)}), f32[256,256]{1,0:T(8,128)}) %all-reduce.14.cloned.1.call-update) | async-done | bytes 262160 | tf_op jit(solution)/shard_map/psum | solution.py:53
  680.8 12.8 %while.54 = (s32[]{:T(128)}, f32[256,256]{0,1:T(8,128)S(1)}, s32[]{:T(128)}) while((s32[]{:T(128)}, f32[256,256]{0,1:T(8,128)S(1)}, s32[]{:T(128)}) %tuple.97), condition=%wide.region_19.21_spmd, body=%wide.region_18.20_spmd.sunk | while | flops 402849792 | bytes 1835053 | solution.py:34
  (238 shorter events, 112.6 us)
Async XLA Ops:
  6.5 15.2 %copy-start = (f32[2048,128]{1,0:T(8,128)S(1)}, f32[2048,128]{1,0:T(8,128)}, u32[]{:S(2)}) copy-start(f32[2048,128]{1,0:T(8,128)} %param.14) | copy-start | bytes 3145732
  6.5 105.0 %all-reduce.6.cloned.1.call-start = ((), (), s32[]{:S(2)}) async-start(), calls=%async_computation.4 | async-start | bytes 524288 | tf_op jit(solution)/shard_map/psum | solution.py:53
  6.5 15.1 %collective-permute-start = (f32[2048,128]{1,0:T(8,128)}, f32[2048,128]{1,0:T(8,128)S(1)}, u32[]{:S(2)}, u32[]{:S(2)}) collective-permute-start(f32[2048,128]{1,0:T(8,128)} %param.14), channel_id=1, source_target_pairs={{0,1},{1,2},{2,3},{3,4},{4,5},{5,6},{6,7},{7,0},{8,9},{9,10},{10,1... | collective-permute-start | bytes 3145736 | tf_op jit(solution)/shard_map/ppermute | solution.py:17
  26.2 216.1 %all-reduce.8.cloned.1.call-start = ((), (), s32[]{:S(2)}) async-start(), calls=%async_computation.5 | async-start | bytes 524288 | tf_op jit(solution)/shard_map/psum | solution.py:53
  132.9 24.0 %collective-permute-start.1 = (f32[2048,128]{0,1:T(8,128)S(1)}, f32[2048,128]{0,1:T(8,128)S(1)}, u32[]{:S(2)}, u32[]{:S(2)}) collective-permute-start(f32[2048,128]{0,1:T(8,128)S(1)} %fusion.27), channel_id=1, source_target_pairs={{0,2},{1,3},{2,4},{3,5},{4,6},{5,7},{6,0},{7,1},{8,10},{9,11},{10,... | collective-permute-start | bytes 3145736 | tf_op jit(solution)/shard_map/ppermute | solution.py:17
  159.5 213.8 %all-reduce.10.cloned.1.call-start = ((), (), s32[]{:S(2)}) async-start(), calls=%async_computation.6 | async-start | bytes 524288 | tf_op jit(solution)/shard_map/psum | solution.py:53
  262.6 28.4 %collective-permute-start.2 = (f32[2048,128]{0,1:T(8,128)S(1)}, f32[2048,128]{0,1:T(8,128)S(1)}, u32[]{:S(2)}, u32[]{:S(2)}) collective-permute-start(f32[2048,128]{0,1:T(8,128)S(1)} %fusion.16), channel_id=1, source_target_pairs={{0,3},{1,4},{2,5},{3,6},{4,7},{5,0},{6,1},{7,2},{8,11},{9,12},{10,... | collective-permute-start | bytes 3145736 | tf_op jit(solution)/shard_map/ppermute | solution.py:17
  392.3 10.9 %copy-start.1 = (s32[2,8]{1,0:T(2,128)S(1)}, s32[2,8]{1,0:T(2,128)}, u32[]{:S(2)}) copy-start(s32[2,8]{1,0:T(2,128)} %param.15) | copy-start | bytes 196
  396.9 21.5 %all-to-all-start = ((f32[8,256,128]{2,1,0:T(8,128)}), f32[8,256,128]{2,1,0:T(8,128)S(1)}, u32[]{:S(2)}, u32[]{:S(2)}) async-start(f32[8,256,128]{2,1,0:T(8,128)} %bitcast.8), calls=%async_computation | async-start | bytes 2097152 | tf_op jit(solution)/shard_map/all_to_all | solution.py:46
  403.2 120.9 %all-reduce.12.cloned.1.call-start = ((), (), s32[]{:S(2)}) async-start(), calls=%async_computation.7 | async-start | bytes 524288 | tf_op jit(solution)/shard_map/psum | solution.py:53
  547.2 21.5 %all-to-all-start.2 = ((f32[8,256,128]{2,1,0:T(8,128)}), f32[8,256,128]{2,1,0:T(8,128)S(1)}, u32[]{:S(2)}, u32[]{:S(2)}) async-start(f32[8,256,128]{2,1,0:T(8,128)} %bitcast.10), calls=%async_computation.2 | async-start | bytes 2097152 | tf_op jit(solution)/shard_map/all_to_all | solution.py:46
  553.6 121.0 %all-reduce.14.cloned.1.call-start = ((), (), s32[]{:S(2)}) async-start(), calls=%async_computation.8 | async-start | bytes 524288 | tf_op jit(solution)/shard_map/psum | solution.py:53
Sparse Core Ops, SparseCore 0:
  26.3 85.2 all-reduce.5
  159.6 82.5 all-reduce.7
  293.7 79.6 all-reduce.9
  443.6 80.4 all-reduce.11
  594.0 80.5 all-reduce.13
where the time goes:
time: 713 us; the launch traced here: 704 us
  waiting for transfers between devices  497 us (70%)
  matrix products  97.6 us (14%)
  blocking collectives  37.1 us (5%)
  starting transfers between devices  22.4 us (3%)
  between operations  17.1 us (2%)
  local copies, waits for them, and re-layouts  16 us (2%)
  other arithmetic  14.5 us (2%)
    psum x5, waiting for transfers between devices, body(): gram_sum = lax.psum(local_gram, 'rows')  409 us
    ppermute x3, waiting for transfers between devices, from_behind(): lax.ppermute(array, axis, [(i, (i + by) % count) for i in range(count)])  58.3 us
    all_to_all x2, blocking collectives, body(): lax.all_to_all(chosen, 'cols', split_axis=0, concat_axis=0, tiled=True)  37.1 us
    dot_general x60, matrix products, advance(): return 1.5 * current - 0.5 * jnp.dot(current, inner, precision=highest)  35.9 us
    all_to_all x2, waiting for transfers between devices, body(): lax.all_to_all(pieces, 'cols', split_axis=0, concat_axis=0, tiled=True)  30.1 us
    dot_general x60, matrix products, advance(): inner = jnp.dot(current.T, current, precision=highest)  24.4 us
    dot_general x5, matrix products, body(): local_gram = jnp.einsum('ra,rb->ab', paired, paired, precision=highest)  21.2 us
    dot_general x5, matrix products, body(): current = jnp.dot(paired, rotation[:, width:], precision=highest)  16.2 us
  transfers between devices with their start and end apart: 10, of which 10 were waited for; matrix products, arithmetic and copies ran while one was open for 0% of the time, Pallas kernels for 0%

commit v1 on v0

v1 whole, which is shorter than its diff:
```python
import functools
import jax, jax.numpy as jnp
from jax import lax
from jax.experimental import pallas as pl
from jax.experimental.pallas import tpu as pltpu
from jax.sharding import PartitionSpec as P

F32=jnp.float32; BF=jnp.bfloat16
W=128; NB=8; STEPS=12; MEET=5
EPS=1e-6

def split(x):
    h=x.astype(BF)
    return h,(x-h.astype(F32)).astype(BF)
def dot3(a,b):
    ah,al=a; bh,bl=b
    return jnp.dot(jnp.concatenate([ah,ah,al],1),jnp.concatenate([bh,bl,bh],0),preferred_element_type=F32)
def dot_nt(a,b):
    return lax.dot_general(a,b,(((1,),(1,)),((),())),preferred_element_type=F32)

def start(aa,ab,ba,bb):
    g=jnp.concatenate([jnp.concatenate([aa,ab],1),jnp.concatenate([ba,bb],1)],0)
    r=lax.broadcasted_iota(jnp.int32,g.shape,0); c=lax.broadcasted_iota(jnp.int32,g.shape,1)
    d=jnp.where(r==c,g,0.0)
    col=lax.rsqrt(jnp.sum(d,axis=1,keepdims=True)+EPS)
    row=lax.rsqrt(jnp.sum(d,axis=0,keepdims=True)+EPS)
    n=g*col*row
    k=jnp.where(r<c,n,jnp.where(r>c,-n,1.0))
    t=jnp.sum(jnp.sum(k*k,axis=1,keepdims=True),axis=0,keepdims=True)
    return k/jnp.sqrt(t)

def advance(x_ref,p):
    x=x_ref[p]
    s=split(x)
    h,l=s
    cross=dot_nt(h,l)
    inner=dot_nt(h,h)+(cross+cross.T)
    x_ref[p]=1.5*x-0.5*dot3(split(inner),s)

def partner(tab,m,j):
    return jnp.where(m<3,lax.rem(j-m-1+NB,NB),tab[jnp.maximum(m-3,0),j])

def meet_kernel(tab,gs,b_in,b_out,g,t,x,q,qt,bb, *, group=8, parts=('ns','gu','ap')):
    for j in range(NB):
        for i in range(NB):
            d=(j-i)%NB
            if d<=4:
                blk=gs[j%2,j//2,d]
            else:
                blk=gs[i%2,i//2,NB-d].T
            g[0,j,i*W:(i+1)*W,:]=blk
        bb[0,j]=b_in[j]
    def meeting(m,_):
        now=lax.rem(m,2); then=1-now
        def off(v): return pl.ds(pl.multiple_of(v*W,W),W)
        for j0 in range(0,NB,group):
            for j in range(j0,j0+group):
                qq=partner(tab,m,j)
                x[j]=start(g[now,qq,off(qq),:],g[now,j,off(qq),:],g[now,qq,j*W:(j+1)*W,:],g[now,j,j*W:(j+1)*W,:])
            if 'ns' in parts:
                def step(_,c):
                    for j in range(j0,j0+group): advance(x,j)
                    return c
                lax.fori_loop(0,STEPS,step,0)
        for j in range(NB):
            qq=partner(tab,m,j)
            w=x[j,:,W:]
            wh,wl=split(w)
            if 'ap' in parts:
                pair=jnp.concatenate([bb[now,qq],bb[now,j]],1)
                bb[then,j]=dot3(split(pair),(wh,wl))
            if 'gu' in parts:
                pair=jnp.concatenate([g[now,qq],g[now,j]],1)
                t[j]=dot3(split(pair),(wh,wl))
        if 'gu' in parts:
            for i in range(NB):
                qi=partner(tab,m,i)
                wt=x[i,:,W:].T
                ws=split(wt)
                rhs=jnp.concatenate([jnp.concatenate([t[j,off(qi),:],t[j,i*W:(i+1)*W,:]],0) for j in range(NB)],1)
                o=dot3(ws,split(rhs))
                for j in range(NB):
                    g[then,j,i*W:(i+1)*W,:]=o[:,j*W:(j+1)*W]
        return 0
    lax.fori_loop(0,MEET,meeting,0)
    b_out[...]=bb[MEET%2]

def meetings(tab,gs,b,**kw):
    V=pl.BlockSpec(memory_space=pltpu.VMEM)
    return pl.pallas_call(functools.partial(meet_kernel,**kw),
        out_shape=jax.ShapeDtypeStruct(b.shape,F32),
        in_specs=[pl.BlockSpec(memory_space=pltpu.SMEM),V,V],out_specs=V,
        scratch_shapes=[pltpu.VMEM((2,NB,NB*W,W),F32),pltpu.VMEM((NB,NB*W,W),F32),pltpu.VMEM((NB,2*W,2*W),F32),
          pltpu.VMEM((8,128),F32),pltpu.VMEM((8,128),F32),pltpu.VMEM((2,)+b.shape,F32)],
        compiler_params=pltpu.CompilerParams(vmem_limit_bytes=56*2**20))(tab,gs,b)


MESH = pl.DeviceIdType.MESH
SIDE = 4
SLAB = 512
HALF = SLAB // 2
SPAN = 5 * W
ROWS = 4 * SPAN
PARTS = ((0, 1024, (0, 1, 2)), (1024, 1024, (1, 2, 0)), (2048, 512, (2, 0, 1)))


def place():
    r, k = lax.axis_index("rows"), lax.axis_index("cols")
    return (lax.rem(r, SIDE), r // SIDE, k // 2), lax.rem(k, 2), k


def device(at, core):
    return (at[1] * SIDE + at[0], at[2] * 2 + core)


def moved(at, axis, by):
    new = list(at)
    new[axis] = lax.rem(at[axis] + by, SIDE)
    return tuple(new)


def greet(peers):
    barrier = pltpu.get_barrier_semaphore()
    for peer in peers:
        pl.semaphore_signal(barrier, inc=1, device_id=peer, device_id_type=MESH)
    pl.semaphore_wait(barrier, len(peers))


def remote(src, dst, send, recv, to):
    return pltpu.make_async_remote_copy(
        src_ref=src, dst_ref=dst, send_sem=send, recv_sem=recv, device_id=to, device_id_type=MESH
    )


def rows_at(start, size, unit):
    return pl.ds(pl.multiple_of(start, unit), size)


def gram_kernel(a, gs, b_out, b, high, low, part, land, *sems):
    (a_send, a_recv, f_send, f_recv, r_send, r_recv, g_send, g_recv, s_send, s_recv) = sems
    at, core, k = place()
    z = at[2]
    sibling = device(at, 1 - core)
    greet([device(moved(at, axis, by), core) for axis in range(3) for by in (1, 2, 3)] + [sibling])
    pending = []

    def go(copy):
        copy.start()
        pending.append(copy)
        return copy

    arrivals = []
    for by in (1, 2, 3):
        to = moved(at, 2, by)
        arrivals.append(go(remote(
            a.at[rows_at(to[2] * SLAB, SLAB, SLAB)], b.at[k], a_send.at[by - 1], a_recv.at[by - 1], device(to, core)
        )))
    own = rows_at(z * SLAB, SLAB, SLAB)
    across = [go(remote(a.at[own], b.at[k], f_send.at[0], f_recv.at[0], sibling))]

    def settle(block, value):
        h, l = split(value)
        high[block] = h
        low[block] = l

    settle(k, a[own, :])
    b_out[k] = a[rows_at(z * SLAB + core * HALF, HALF, HALF), :]

    def half_of(block):
        b_out[block] = b[block, rows_at(core * HALF, HALF, HALF), :]

    for by in (1, 2, 3):
        block = lax.rem(z + SIDE - by, SIDE) * 2 + core
        arrivals[by - 1].wait_recv()
        across.append(go(remote(b.at[block], b.at[block], f_send.at[by], f_recv.at[by], sibling)))
        settle(block, b[block])
        half_of(block)
    for by in range(4):
        block = lax.rem(z + SIDE - by, SIDE) * 2 + 1 - core
        across[by].wait_recv()
        settle(block, b[block])
        half_of(block)

    for t in range(4):
        j = 2 * t + core
        ids = [lax.rem(j - d + NB, NB) for d in range(5)]
        lh = jnp.concatenate([high[i] for i in ids], 1)
        ll = jnp.concatenate([low[i] for i in ids], 1)
        rh, rl = high[j], low[j]
        part[t * SPAN:(t + 1) * SPAN, :] = lax.dot_general(
            jnp.concatenate([lh, lh, ll], 0), jnp.concatenate([rh, rl, rh], 0),
            (((0,), (0,)), ((), ())), preferred_element_type=F32,
        )

    base = [p[0] for p in PARTS]
    size = [p[1] for p in PARTS]

    def spread(p, stage):
        axis, n = PARTS[p][2][stage], size[p] // 4
        copies = []
        for by in (1, 2, 3):
            to = moved(at, axis, by)
            copies.append(go(remote(
                part.at[rows_at(base[p] + to[axis] * n, n, 8)], land.at[p, stage, by - 1, pl.ds(0, n)],
                r_send.at[p, stage, by - 1], r_recv.at[p, stage, by - 1], device(to, core),
            )))
        base[p] = base[p] + at[axis] * n
        size[p] = n
        return copies

    waiting = [spread(p, 0) for p in range(3)]
    for stage in range(3):
        for p in range(3):
            for copy in waiting[p]:
                copy.wait_recv()
            n, mine = size[p], rows_at(base[p], size[p], 8)
            total = part[mine, :]
            for by in range(3):
                total = total + land[p, stage, by, 0:n, :]
            if stage < 2:
                part[mine, :] = total
                waiting[p] = spread(p, stage + 1)
            else:
                gs[core, mine, :] = total

    def share(p, stage):
        axis, mine = PARTS[p][2][stage], rows_at(base[p], size[p], 8)
        copies = []
        for by in (1, 2, 3):
            copies.append(go(remote(
                gs.at[core, mine], gs.at[core, mine], g_send.at[p, stage, by - 1], g_recv.at[p, stage, by - 1],
                device(moved(at, axis, by), core),
            )))
        base[p] = base[p] - at[axis] * size[p]
        size[p] = size[p] * 4
        return copies

    waiting = [share(p, 2) for p in range(3)]
    last = []
    for stage in (1, 0, -1):
        for p in range(3):
            for copy in waiting[p]:
                copy.wait_recv()
            if stage >= 0:
                waiting[p] = share(p, stage)
            else:
                whole = pl.ds(PARTS[p][0], PARTS[p][1])
                last.append(go(remote(gs.at[core, whole], gs.at[core, whole], s_send.at[p], s_recv.at[p], sibling)))
    for copy in last:
        copy.wait_recv()
    for copy in pending:
        copy.wait_send()


def gram_of(a):
    vmem = pl.BlockSpec(memory_space=pltpu.VMEM)
    dma = pltpu.SemaphoreType.DMA
    return pl.pallas_call(
        gram_kernel,
        out_shape=(
            jax.ShapeDtypeStruct((2, ROWS, W), F32),
            jax.ShapeDtypeStruct((NB, HALF, W), F32),
        ),
        in_specs=[vmem],
        out_specs=(vmem, vmem),
        scratch_shapes=[
            pltpu.VMEM((NB, SLAB, W), F32),
            pltpu.VMEM((NB, SLAB, W), BF),
            pltpu.VMEM((NB, SLAB, W), BF),
            pltpu.VMEM((ROWS, W), F32),
            pltpu.VMEM((3, 3, 3, 256, W), F32),
            dma((3,)), dma((3,)), dma((4,)), dma((4,)),
            dma((3, 3, 3)), dma((3, 3, 3)), dma((3, 3, 3)), dma((3, 3, 3)), dma((3,)), dma((3,)),
        ],
        compiler_params=pltpu.CompilerParams(
            collective_id=0, has_side_effects=True, vmem_limit_bytes=48 * 2**20
        ),
    )(a)


def return_kernel(b, out, send, recv):
    at, core, k = place()
    row = at[1] * SIDE + at[0]
    peers = [lax.rem(k + by, NB) for by in range(1, NB)]
    greet([(row, peer) for peer in peers])
    mine = rows_at(k * HALF, HALF, HALF)
    copies = []
    for n, peer in enumerate(peers):
        copies.append(remote(b.at[peer], out.at[mine], send.at[n], recv.at[n], (row, peer)))
        copies[-1].start()
    out[mine, :] = b[k]
    for copy in copies:
        copy.wait()


def returned(b):
    vmem = pl.BlockSpec(memory_space=pltpu.VMEM)
    dma = pltpu.SemaphoreType.DMA
    return pl.pallas_call(
        return_kernel,
        out_shape=jax.ShapeDtypeStruct((NB * HALF, W), F32),
        in_specs=[vmem],
        out_specs=vmem,
        scratch_shapes=[dma((NB - 1,)), dma((NB - 1,))],
        compiler_params=pltpu.CompilerParams(
            collective_id=1, has_side_effects=True, vmem_limit_bytes=32 * 2**20
        ),
    )(b)


def body(matrix, partners):
    gs, b = gram_of(matrix)
    return returned(meetings(partners, gs.reshape(2, 4, 5, W, W), b))


def solution(mesh):
    placed = (P("rows", "cols"), P())
    return jax.shard_map(
        body, mesh=mesh, in_specs=placed, out_specs=P("rows", "cols"), check_vma=False
    )
```

time: 713 us -> 255 us (0.36); the launches traced: 704 us -> 255 us
  waiting for transfers between devices: 497 us -> 0 us
  Pallas kernels: 0 us -> 249 us
  matrix products: 97.6 us -> 0 us
  blocking collectives: 37.1 us -> 0 us
  starting transfers between devices: 22.4 us -> 0 us
  between operations: 17.1 us -> 0.03 us
  other arithmetic: 14.5 us -> 0 us
  local copies, waits for them, and re-layouts: 16 us -> 5.88 us
    psum x5 -> x0, waiting for transfers between devices: 409 us -> none  [body(): gram_sum = lax.psum(local_gram, 'rows')]
    pallas_call x0 -> x3, Pallas kernels: none -> 249 us  [the longest x1 175 us: meetings(): pl.pallas_call(functools.partial(meet_kernel, **kw), out_shape=jax.ShapeD...]
    dot_general x130 -> x0, matrix products: 97.6 us -> none  [the longest x60 35.9 us: advance(): return 1.5 * current - 0.5 * jnp.dot(current, inner, precision=highest)]
    ppermute x3 -> x0, waiting for transfers between devices: 58.3 us -> none  [from_behind(): lax.ppermute(array, axis, [(i, (i + by) % count) for i in range(count)])]
    all_to_all x2 -> x0, blocking collectives: 37.1 us -> none  [body(): lax.all_to_all(chosen, 'cols', split_axis=0, concat_axis=0, tiled=True)]
    all_to_all x2 -> x0, waiting for transfers between devices: 30.1 us -> none  [body(): lax.all_to_all(pieces, 'cols', split_axis=0, concat_axis=0, tiled=True)]
    gather x7 -> x0, local copies, waits for them, and re-layouts: 14.1 us -> none  [the longest x5 12.8 us: start_iterate(): scale = lax.rsqrt(jnp.diagonal(gram_full) + epsilon)]
    all_to_all x2 -> x0, starting transfers between devices: 12.7 us -> none  [body(): lax.all_to_all(pieces, 'cols', split_axis=0, concat_axis=0, tiled=True)]
  transfers between devices with their start and end apart: 10 -> 0, of which waited for: 10 -> 0; matrix products, arithmetic and copies ran while one was open for 0% -> 0% of each run, Pallas kernels for 0% -> 0%
where the time goes in v1:
time: 255 us
  Pallas kernels  249 us (98%)
  local copies, waits for them, and re-layouts  5.88 us (2%)
    pallas_call x1, Pallas kernels, meetings(): pl.pallas_call(functools.partial(meet_kernel, **kw), out_shape=jax.ShapeD...  175 us
    pallas_call x1, Pallas kernels, gram_of(): pl.pallas_call(gram_kernel, out_shape=(jax.ShapeDtypeStruct((2, ROWS, W),...  57.9 us
    pallas_call x1, Pallas kernels, returned(): pl.pallas_call(return_kernel, out_shape=jax.ShapeDtypeStruct((NB * HALF,...  15.7 us
    unnamed x9, local copies, waits for them, and re-layouts  5.88 us

profile of v1, /device:TPU:1, one launch (start us, length us, event | category | flops | bytes accessed | tf_op | source)
XLA Modules:
  0.0 254.8 jit_solution(15204848821440998412)
XLA Ops:
  0.0 0.0 copy-start.3
  0.0 1.2 copy-done.3
  1.2 57.9 %shard_map.28 = (f32[2,2560,128]{2,1,0:T(8,128)S(1)}, f32[8,256,128]{2,1,0:T(8,128)S(1)}) custom-call(f32[2048,128]{1,0:T(8,128)S(1)} %copy-done.3), custom_call_target="tpu_custom_call" | custom-call | tf_op jit(solution)/shard_map/pallas_call | solution.py:258
  59.2 0.0 copy-start.1
  59.2 1.5 copy-done.1
  60.6 0.0 copy-start.2
  60.7 1.0 copy-done.2
  61.6 175.3 %shard_map.29.b = f32[8,256,128]{2,1,0:T(8,128)} custom-call(s32[2,8]{1,0:T(2,128)} %tab.1, f32[2,4,5,128,128]{4,3,2,1,0:T(8,128)} %bitcast.1, f32[8,256,128]{2,1,0:T(8,128)} %copy-done.2), custom_call_target="tpu_custom_call" | custom-call | tf_op jit(solution)/shard_map/pallas_call | solution.py:90
  236.9 0.0 copy-start
  236.9 1.2 copy-done
  238.1 15.7 %shard_map.30 = f32[2048,128]{1,0:T(8,128)S(1)} custom-call(f32[8,256,128]{2,1,0:T(8,128)S(1)} %copy-done), custom_call_target="tpu_custom_call" | custom-call | tf_op jit(solution)/shard_map/pallas_call | solution.py:299
  253.9 1.0 copy.4
Async XLA Ops:
  0.0 1.2 copy-start.3
  59.2 1.5 copy-start.1
  60.6 1.0 copy-start.2
  236.9 1.2 copy-start

commit v2 on v1

--- a/solution.py
+++ b/solution.py
@@ -6,7 +6,7 @@
 from jax.sharding import PartitionSpec as P
 
 F32=jnp.float32; BF=jnp.bfloat16
-W=128; NB=8; STEPS=12; MEET=5
+W=128; NB=8; STEPS=12; CYCLE=3; MEET=5
 EPS=1e-6
 
 def split(x):
@@ -36,64 +36,6 @@
     cross=dot_nt(h,l)
     inner=dot_nt(h,h)+(cross+cross.T)
     x_ref[p]=1.5*x-0.5*dot3(split(inner),s)
-
-def partner(tab,m,j):
-    return jnp.where(m<3,lax.rem(j-m-1+NB,NB),tab[jnp.maximum(m-3,0),j])
-
-def meet_kernel(tab,gs,b_in,b_out,g,t,x,q,qt,bb, *, group=8, parts=('ns','gu','ap')):
-    for j in range(NB):
-        for i in range(NB):
-            d=(j-i)%NB
-            if d<=4:
-                blk=gs[j%2,j//2,d]
-            else:
-                blk=gs[i%2,i//2,NB-d].T
-            g[0,j,i*W:(i+1)*W,:]=blk
-        bb[0,j]=b_in[j]
-    def meeting(m,_):
-        now=lax.rem(m,2); then=1-now
-        def off(v): return pl.ds(pl.multiple_of(v*W,W),W)
-        for j0 in range(0,NB,group):
-            for j in range(j0,j0+group):
-                qq=partner(tab,m,j)
-                x[j]=start(g[now,qq,off(qq),:],g[now,j,off(qq),:],g[now,qq,j*W:(j+1)*W,:],g[now,j,j*W:(j+1)*W,:])
-            if 'ns' in parts:
-                def step(_,c):
-                    for j in range(j0,j0+group): advance(x,j)
-                    return c
-                lax.fori_loop(0,STEPS,step,0)
-        for j in range(NB):
-            qq=partner(tab,m,j)
-            w=x[j,:,W:]
-            wh,wl=split(w)
-            if 'ap' in parts:
-                pair=jnp.concatenate([bb[now,qq],bb[now,j]],1)
-                bb[then,j]=dot3(split(pair),(wh,wl))
-            if 'gu' in parts:
-                pair=jnp.concatenate([g[now,qq],g[now,j]],1)
-                t[j]=dot3(split(pair),(wh,wl))
-        if 'gu' in parts:
-            for i in range(NB):
-                qi=partner(tab,m,i)
-                wt=x[i,:,W:].T
-                ws=split(wt)
-                rhs=jnp.concatenate([jnp.concatenate([t[j,off(qi),:],t[j,i*W:(i+1)*W,:]],0) for j in range(NB)],1)
-                o=dot3(ws,split(rhs))
-                for j in range(NB):
-                    g[then,j,i*W:(i+1)*W,:]=o[:,j*W:(j+1)*W]
-        return 0
-    lax.fori_loop(0,MEET,meeting,0)
-    b_out[...]=bb[MEET%2]
-
-def meetings(tab,gs,b,**kw):
-    V=pl.BlockSpec(memory_space=pltpu.VMEM)
-    return pl.pallas_call(functools.partial(meet_kernel,**kw),
-        out_shape=jax.ShapeDtypeStruct(b.shape,F32),
-        in_specs=[pl.BlockSpec(memory_space=pltpu.SMEM),V,V],out_specs=V,
-        scratch_shapes=[pltpu.VMEM((2,NB,NB*W,W),F32),pltpu.VMEM((NB,NB*W,W),F32),pltpu.VMEM((NB,2*W,2*W),F32),
-          pltpu.VMEM((8,128),F32),pltpu.VMEM((8,128),F32),pltpu.VMEM((2,)+b.shape,F32)],
-        compiler_params=pltpu.CompilerParams(vmem_limit_bytes=56*2**20))(tab,gs,b)
-
 
 MESH = pl.DeviceIdType.MESH
 SIDE = 4
@@ -278,39 +220,120 @@
     )(a)
 
 
-def return_kernel(b, out, send, recv):
+def partner(table, meeting, j):
+    if meeting < CYCLE:
+        return lax.rem(j - meeting - 1 + NB, NB)
+    return table[meeting - CYCLE, j]
+
+
+def column(g, j):
+    first = j * NB
+    return jnp.concatenate([g[first + i] for i in range(NB)], 0)
+
+
+def corner(g, i, j):
+    return g[j * NB + i]
+
+
+def meet_kernel(table, gs, b_in, out, g0, g1, g2, g3, g4, x, q, t, b0, b1, q_send, q_recv, g_send, g_recv, o_send, o_recv):
     at, core, k = place()
     row = at[1] * SIDE + at[0]
     peers = [lax.rem(k + by, NB) for by in range(1, NB)]
     greet([(row, peer) for peer in peers])
+    sibling = device(at, 1 - core)
+    pending = []
+
+    def go(copy):
+        copy.start()
+        pending.append(copy)
+        return copy
+
+    grams = (g0, g1, g2, g3, g4)
+    for j in range(NB):
+        for i in range(NB):
+            d = (j - i) % NB
+            g0[j * NB + i] = (
+                gs[j % 2, j // 2, d] if d <= 4 else gs[i % 2, i // 2, NB - d].T
+            )
+    b_now, b_then = b_in, b0
+    for m in range(MEET):
+        g = grams[m]
+        for n in range(4):
+            j = 2 * n + core
+            qq = partner(table, m, j)
+            x[n] = start(corner(g, qq, qq), corner(g, qq, j), corner(g, j, qq), corner(g, j, j))
+
+        def step(_, carry):
+            for n in range(4):
+                advance(x, n)
+            return carry
+
+        lax.fori_loop(0, STEPS, step, 0)
+        q[m, core] = x[:, :, W:]
+        swap = go(remote(q.at[m, core], q.at[m, core], q_send.at[m], q_recv.at[m], sibling))
+
+        def project(n, m=m, g=g):
+            j = 2 * n + core
+            pair = jnp.concatenate([column(g, partner(table, m, j)), column(g, j)], 1)
+            t[n * NB:(n + 1) * NB] = dot3(split(pair), split(q[m, core, n])).reshape(NB, W, W)
+
+        if m < MEET - 1:
+            for n in range(4):
+                project(n)
+        swap.wait_recv()
+        if m < MEET - 1:
+            turned = [split(q[m, i % 2, i // 2].T) for i in range(NB)]
+            arriving = []
+            for n in range(4):
+                for i in range(NB):
+                    pair = jnp.concatenate([t[n * NB + partner(table, m, i)], t[n * NB + i]], 0)
+                    grams[m + 1][(2 * n + core) * NB + i] = dot3(turned[i], split(pair))
+                done = grams[m + 1].at[pl.ds((2 * n + core) * NB, NB)]
+                arriving.append(go(remote(done, done, g_send.at[m, n], g_recv.at[m, n], sibling)))
+        for j in range(NB):
+            pair = jnp.concatenate([b_now[partner(table, m, j)], b_now[j]], 1)
+            b_then[j] = dot3(split(pair), split(q[m, j % 2, j // 2]))
+        if m < MEET - 1:
+            for copy in arriving:
+                copy.wait_recv()
+        b_now, b_then = (b0, b1) if b_then is b0 else (b1, b0)
     mine = rows_at(k * HALF, HALF, HALF)
-    copies = []
-    for n, peer in enumerate(peers):
-        copies.append(remote(b.at[peer], out.at[mine], send.at[n], recv.at[n], (row, peer)))
-        copies[-1].start()
-    out[mine, :] = b[k]
-    for copy in copies:
-        copy.wait()
-
-
-def returned(b):
+    returning = [
+        go(remote(b_now.at[peer], out.at[mine], o_send.at[n], o_recv.at[n], (row, peer)))
+        for n, peer in enumerate(peers)
+    ]
+    out[mine, :] = b_now[k]
+    for copy in returning:
+        copy.wait_recv()
+    for copy in pending:
+        copy.wait_send()
+
+
+def meetings(table, gs, b):
     vmem = pl.BlockSpec(memory_space=pltpu.VMEM)
     dma = pltpu.SemaphoreType.DMA
     return pl.pallas_call(
-        return_kernel,
+        meet_kernel,
         out_shape=jax.ShapeDtypeStruct((NB * HALF, W), F32),
-        in_specs=[vmem],
+        in_specs=[pl.BlockSpec(memory_space=pltpu.SMEM), vmem, vmem],
         out_specs=vmem,
-        scratch_shapes=[dma((NB - 1,)), dma((NB - 1,))],
+        scratch_shapes=[pltpu.VMEM((NB * NB, W, W), F32)] * 5 + [
+            pltpu.VMEM((4, 2 * W, 2 * W), F32),
+            pltpu.VMEM((MEET, 2, 4, 2 * W, W), F32),
+            pltpu.VMEM((4 * NB, W, W), F32),
+            pltpu.VMEM((NB, HALF, W), F32),
+            pltpu.VMEM((NB, HALF, W), F32),
+            dma((MEET,)), dma((MEET,)), dma((MEET - 1, 4)), dma((MEET - 1, 4)), dma((NB - 1,)), dma((NB - 1,)),
+        ],
         compiler_params=pltpu.CompilerParams(
-            collective_id=1, has_side_effects=True, vmem_limit_bytes=32 * 2**20
+            collective_id=1, has_side_effects=True, vmem_limit_bytes=56 * 2**20
         ),
-    )(b)
+    )(table, gs, b)
 
 
 def body(matrix, partners):
     gs, b = gram_of(matrix)
-    return returned(meetings(partners, gs.reshape(2, 4, 5, W, W), b))
+    return meetings(partners, gs.reshape(2, 4, 5, W, W), b)
 
 
 def solution(mesh):

time: 255 us -> 188 us (0.74)
  Pallas kernels: 249 us -> 182 us
    pallas_call x2 -> x1, Pallas kernels: 191 us -> 124 us  [meetings(): pl.pallas_call(meet_kernel, out_shape=jax.ShapeDtypeStruct((NB * HALF, W)...]
    unnamed x9 -> x7, local copies, waits for them, and re-layouts: 5.88 us -> 5.95 us
where the time goes in v2:
time: 188 us
  Pallas kernels  182 us (97%)
  local copies, waits for them, and re-layouts  5.95 us (3%)
    pallas_call x1, Pallas kernels, meetings(): pl.pallas_call(meet_kernel, out_shape=jax.ShapeDtypeStruct((NB * HALF, W)...  124 us
    pallas_call x1, Pallas kernels, gram_of(): pl.pallas_call(gram_kernel, out_shape=(jax.ShapeDtypeStruct((2, ROWS, W),...  57.9 us
    unnamed x7, local copies, waits for them, and re-layouts  5.95 us

profile of v2, /device:TPU:1, one launch (start us, length us, event | category | flops | bytes accessed | tf_op | source)
XLA Modules:
  0.0 187.9 jit_solution(2503479131133656652)
XLA Ops:
  0.0 0.0 copy-start.2
  0.0 1.2 copy-done.2
  1.2 57.9 %shard_map.28 = (f32[2,2560,128]{2,1,0:T(8,128)S(1)}, f32[8,256,128]{2,1,0:T(8,128)S(1)}) custom-call(f32[2048,128]{1,0:T(8,128)S(1)} %copy-done.2), custom_call_target="tpu_custom_call" | custom-call | tf_op jit(solution)/shard_map/pallas_call | solution.py:200
  59.2 0.0 copy-start
  59.2 1.5 copy-done
  60.7 0.0 copy-start.1
  60.7 1.0 copy-done.1
  61.6 124.1 %shard_map.29 = f32[2048,128]{1,0:T(8,128)} custom-call(s32[2,8]{1,0:T(2,128)} %table.1, f32[2,4,5,128,128]{4,3,2,1,0:T(8,128)} %bitcast.1, f32[8,256,128]{2,1,0:T(8,128)} %copy-done.1), custom_call_target="tpu_custom_call" | custom-call | tf_op jit(solution)/shard_map/pallas_call | solution.py:315
  185.7 2.3 %copy.4 = f32[2048,128]{1,0:T(8,128)} copy(f32[2048,128]{1,0:T(8,128)} %shard_map.29) | data formatting | bytes 2097152
Async XLA Ops:
  0.0 1.2 copy-start.2
  59.2 1.5 copy-start
  60.7 1.0 copy-start.1

commit v3 on v0

v3 whole, which is shorter than its diff:
```python
import jax
import jax.numpy as jnp
from jax import lax
from jax.experimental import pallas as pl
from jax.experimental.pallas import tpu as pltpu
from jax.sharding import PartitionSpec as P

F32, BF = jnp.float32, jnp.bfloat16
MESH = pl.DeviceIdType.MESH
CYCLE = 3
MEET = 5
STEPS = 12
EPS = 1e-6
W = 128
NB = 8
OWN = NB // 2
SIDE = 4
SLAB = 512
HALF = SLAB // 2
NEAR = 5
PART = OWN * W
ROWS = NEAR * PART
ORDERS = ((0, 1, 2), (1, 2, 0), (2, 0, 1), (0, 1, 2), (1, 2, 0))
FIRST, REST = (0, 1), (2, 3, 4)


def split(x):
    high = x.astype(BF)
    return high, (x - high.astype(F32)).astype(BF)


def dot(a, b):
    return jnp.dot(a, b, preferred_element_type=F32)


def dot_nt(a, b):
    return lax.dot_general(a, b, (((1,), (1,)), ((), ())), preferred_element_type=F32)


def dot3(a, b):
    (ah, al), (bh, bl) = a, b
    return dot(jnp.concatenate([ah, ah, al], 1), jnp.concatenate([bh, bl, bh], 0))


def start(aa, ab, ba, bb):
    g = jnp.concatenate([jnp.concatenate([aa, ab], 1), jnp.concatenate([ba, bb], 1)], 0)
    r = lax.broadcasted_iota(jnp.int32, g.shape, 0)
    c = lax.broadcasted_iota(jnp.int32, g.shape, 1)
    diagonal = jnp.where(r == c, g, 0.0)
    tall = lax.rsqrt(jnp.sum(diagonal, axis=1, keepdims=True) + EPS)
    wide = lax.rsqrt(jnp.sum(diagonal, axis=0, keepdims=True) + EPS)
    normed = g * tall * wide
    k = jnp.where(r < c, normed, jnp.where(r > c, -normed, 1.0))
    total = jnp.sum(jnp.sum(k * k, axis=1, keepdims=True), axis=0, keepdims=True)
    return k / jnp.sqrt(total)


def polar_steps(x, count):
    def step(_, carry):
        now = [x[n] for n in range(OWN)]
        halves = [split(v) for v in now]
        crossed = [dot_nt(h, l) for h, l in halves]
        plain = [dot_nt(h, h) for h, _ in halves]
        inner = [split(p + (c + c.T)) for p, c in zip(plain, crossed)]
        outer = [dot3(i, h) for i, h in zip(inner, halves)]
        for n in range(OWN):
            x[n] = 1.5 * now[n] - 0.5 * outer[n]
        return carry

    lax.fori_loop(0, count, step, 0, unroll=2)


def place():
    r, k = lax.axis_index("rows"), lax.axis_index("cols")
    return (lax.rem(r, SIDE), r // SIDE, k // 2), lax.rem(k, 2), k


def device(at, core):
    return (at[1] * SIDE + at[0], at[2] * 2 + core)


def moved(at, axis, by):
    new = list(at)
    new[axis] = lax.rem(at[axis] + by, SIDE)
    return tuple(new)


def greet(peers):
    barrier = pltpu.get_barrier_semaphore()
    for peer in peers:
        pl.semaphore_signal(barrier, inc=1, device_id=peer, device_id_type=MESH)
    pl.semaphore_wait(barrier, len(peers))


def remote(src, dst, send, recv, to):
    return pltpu.make_async_remote_copy(
        src_ref=src, dst_ref=dst, send_sem=send, recv_sem=recv, device_id=to, device_id_type=MESH
    )


def rows_at(start, size, unit):
    return pl.ds(pl.multiple_of(start, unit), size)


def partner(table, meeting, j):
    if meeting < CYCLE:
        return (j + NB - meeting - 1) % NB if isinstance(j, int) else lax.rem(j + NB - meeting - 1, NB)
    return table[meeting - CYCLE, j]


def column(g, j):
    return jnp.concatenate([g[j * NB + i] for i in range(NB)], 0)


def kernel(table, a, out, b, high, low, high_t, low_t, part, land, gs, g0, g1, g2, g3, g4, x, q, th, tl, b0, b1,
           a_send, a_recv, f_send, f_recv, r_send, r_recv, s_send, s_recv, c_send, c_recv,
           q_send, q_recv, g_send, g_recv, o_send, o_recv):
    at, core, k = place()
    row, z = at[1] * SIDE + at[0], at[2]
    sibling = device(at, 1 - core)
    peers = [lax.rem(k + by, NB) for by in range(1, NB)]
    greet([(row, peer) for peer in peers] + [device(moved(at, axis, by), core) for axis in (0, 1) for by in (1, 2, 3)])
    pending = []

    def go(copy):
        copy.start()
        pending.append(copy)
        return copy

    def arrive(copies):
        for copy in copies:
            copy.wait_recv()

    arrivals = []
    for by in (1, 2, 3):
        to = moved(at, 2, by)
        arrivals.append(go(remote(
            a.at[rows_at(to[2] * SLAB, SLAB, SLAB)], b.at[k], a_send.at[by - 1], a_recv.at[by - 1], device(to, core)
        )))
    own = rows_at(z * SLAB, SLAB, SLAB)
    across = [go(remote(a.at[own], b.at[k], f_send.at[0], f_recv.at[0], sibling))]

    def settle(block, value):
        h, l = split(value)
        high[block] = h
        low[block] = l
        high_t[block] = h.T
        low_t[block] = l.T

    settle(k, a[own, :])
    b[k] = a[own, :]
    for by in (1, 2, 3):
        block = lax.rem(z + SIDE - by, SIDE) * 2 + core
        arrivals[by - 1].wait_recv()
        across.append(go(remote(b.at[block], b.at[block], f_send.at[by], f_recv.at[by], sibling)))
        settle(block, b[block])
    for by in range(4):
        block = lax.rem(z + SIDE - by, SIDE) * 2 + 1 - core
        across[by].wait_recv()
        settle(block, b[block])

    for t in range(OWN):
        j = 2 * t + core
        ids = [lax.rem(j - d + NB, NB) for d in range(NEAR)]
        left = jnp.concatenate([jnp.concatenate([high_t[i], high_t[i], low_t[i]], 1) for i in ids], 0)
        column_sum = dot(left, jnp.concatenate([high[j], low[j], high[j]], 0))
        for d in range(NEAR):
            part[d * PART + t * W:d * PART + (t + 1) * W, :] = column_sum[d * W:(d + 1) * W]

    base = [d * PART for d in range(NEAR)]
    size = [PART] * NEAR

    def spread(p, stage):
        axis, n = ORDERS[p][stage], size[p] // SIDE
        copies = []
        for by in (1, 2, 3):
            to = moved(at, axis, by)
            copies.append(go(remote(
                part.at[rows_at(base[p] + to[axis] * n, n, 8)], land.at[p, stage, by - 1, pl.ds(0, n)],
                r_send.at[p, stage, by - 1], r_recv.at[p, stage, by - 1], device(to, core),
            )))
        base[p] = base[p] + at[axis] * n
        size[p] = n
        return copies

    waiting = [spread(p, 0) for p in range(NEAR)]
    for stage in range(3):
        for p in range(NEAR):
            arrive(waiting[p])
            n, mine = size[p], rows_at(base[p], size[p], 8)
            total = part[mine, :]
            for by in range(3):
                total = total + land[p, stage, by, 0:n, :]
            if stage < 2:
                part[mine, :] = total
                waiting[p] = spread(p, stage + 1)
            else:
                gs[core, mine, :] = total

    def share(p, stage):
        axis, mine = ORDERS[p][stage], rows_at(base[p], size[p], 8)
        copies = [
            go(remote(
                gs.at[core, mine], gs.at[core, mine], s_send.at[p, stage, by - 1], s_recv.at[p, stage, by - 1],
                device(moved(at, axis, by), core),
            ))
            for by in (1, 2, 3)
        ]
        base[p] = base[p] - at[axis] * size[p]
        size[p] = size[p] * SIDE
        return copies

    def forward(p, stage):
        arrive(waiting[p])
        if stage >= 0:
            waiting[p] = share(p, stage)
        else:
            whole = pl.ds(p * PART, PART)
            waiting[p] = [go(remote(gs.at[core, whole], gs.at[core, whole], c_send.at[p], c_recv.at[p], sibling))]

    for p in range(NEAR):
        waiting[p] = share(p, 2)
    for p in FIRST + REST:
        forward(p, 1)
    for stage in (0, -1):
        for p in FIRST:
            forward(p, stage)
    for p in FIRST:
        arrive(waiting[p])

    def summed(j, d):
        return gs[lax.rem(j, 2), rows_at(d * PART + (j // 2) * W, W, W), :]

    grams = (g0, g1, g2, g3, g4)
    mine = [2 * n + core for n in range(OWN)]
    for n, j in enumerate(mine):
        before = partner(table, 0, j)
        ab = summed(j, 1)
        x[n] = start(summed(before, 0), ab, ab.T, summed(j, 0))
    polar_steps(x, 4)
    for p in REST:
        forward(p, 0)
    polar_steps(x, 4)
    for p in REST:
        forward(p, -1)
    polar_steps(x, 4)
    for p in REST:
        arrive(waiting[p])
    for j in range(NB):
        for i in range(NB):
            d = (j - i) % NB
            c, e, f = (j, d, j // 2) if d < NEAR else (i, NB - d, i // 2)
            block = gs[c % 2, e * PART + f * W:e * PART + (f + 1) * W, :]
            g0[j * NB + i] = block if d < NEAR else block.T

    half = rows_at(core * HALF, HALF, HALF)
    returning = []
    for m in range(MEET):
        g = grams[m]
        if m:
            for n, j in enumerate(mine):
                other = partner(table, m, j)
                x[n] = start(g[other * NB + other], g[j * NB + other], g[other * NB + j], g[j * NB + j])
            polar_steps(x, STEPS)
        q[m, core] = x[:, :, W:]
        swap = go(remote(q.at[m, core], q.at[m, core], q_send.at[m], q_recv.at[m], sibling))

        def rotated(j, factor, m=m):
            other = partner(table, m, j)
            if m == 0:
                pair = [b[other, half, :], b[j, half, :]]
            else:
                held = (b0, b1)[(m - 1) % 2]
                pair = [held[other], held[j]]
            return dot3(split(jnp.concatenate(pair, 1)), split(factor))

        then = (b0, b1)[m % 2]
        if m < MEET - 1:
            for n, j in enumerate(mine):
                pair = jnp.concatenate([column(g, partner(table, m, j)), column(g, j)], 1)
                h, l = split(dot3(split(pair), split(q[m, core, n])))
                th[n * NB:(n + 1) * NB] = h.reshape(NB, W, W)
                tl[n * NB:(n + 1) * NB] = l.reshape(NB, W, W)
            swap.wait_recv()
            turned = [split(q[m, i % 2, i // 2].T) for i in range(NB)]
            arriving = []
            for two in (0, 2):
                made = []
                for i in range(NB):
                    other = partner(table, m, i)
                    right = tuple(
                        jnp.concatenate([
                            jnp.concatenate([s[n * NB + other], s[n * NB + i]], 0) for n in (two, two + 1)
                        ], 1)
                        for s in (th, tl)
                    )
                    made.append(dot3(turned[i], right))
                for e, n in enumerate((two, two + 1)):
                    for i in range(NB):
                        grams[m + 1][mine[n] * NB + i] = made[i][:, e * W:(e + 1) * W]
                    done = grams[m + 1].at[pl.ds(mine[n] * NB, NB)]
                    arriving.append(go(remote(done, done, g_send.at[m, n], g_recv.at[m, n], sibling)))
            for j in range(NB):
                then[j] = rotated(j, q[m, j % 2, j // 2])
            arrive(arriving)
        else:
            swap.wait_recv()
            home = rows_at(k * HALF, HALF, HALF)
            for n, j in enumerate(peers):
                then[j] = rotated(j, q[m, lax.rem(j, 2), j // 2])
                returning.append(go(remote(then.at[j], out.at[home], o_send.at[n], o_recv.at[n], (row, j))))
            out[home, :] = rotated(k, q[m, core, z])
    arrive(returning)
    for copy in pending:
        copy.wait_send()


def body(matrix, partners):
    vmem = pl.BlockSpec(memory_space=pltpu.VMEM)
    dma = pltpu.SemaphoreType.DMA
    square = (NB * NB, W, W)
    return pl.pallas_call(
        kernel,
        out_shape=jax.ShapeDtypeStruct(matrix.shape, F32),
        in_specs=[pl.BlockSpec(memory_space=pltpu.SMEM), vmem],
        out_specs=vmem,
        scratch_shapes=[
            pltpu.VMEM((NB, SLAB, W), F32),
            pltpu.VMEM((NB, SLAB, W), BF),
            pltpu.VMEM((NB, SLAB, W), BF),
            pltpu.VMEM((NB, W, SLAB), BF),
            pltpu.VMEM((NB, W, SLAB), BF),
            pltpu.VMEM((ROWS, W), F32),
            pltpu.VMEM((NEAR, 3, 3, PART // SIDE, W), F32),
            pltpu.VMEM((2, ROWS, W), F32),
        ] + [pltpu.VMEM(square, F32)] * MEET + [
            pltpu.VMEM((OWN, 2 * W, 2 * W), F32),
            pltpu.VMEM((MEET, 2, OWN, 2 * W, W), F32),
            pltpu.VMEM((OWN * NB, W, W), BF),
            pltpu.VMEM((OWN * NB, W, W), BF),
            pltpu.VMEM((NB, HALF, W), F32),
            pltpu.VMEM((NB, HALF, W), F32),
            dma((3,)), dma((3,)), dma((4,)), dma((4,)),
            dma((NEAR, 3, 3)), dma((NEAR, 3, 3)), dma((NEAR, 3, 3)), dma((NEAR, 3, 3)), dma((NEAR,)), dma((NEAR,)),
            dma((MEET,)), dma((MEET,)), dma((MEET - 1, OWN)), dma((MEET - 1, OWN)), dma((NB - 1,)), dma((NB - 1,)),
        ],
        compiler_params=pltpu.CompilerParams(
            collective_id=0, has_side_effects=True, vmem_limit_bytes=58 * 2**20
        ),
    )(partners, matrix)


def solution(mesh):
    placed = (P("rows", "cols"), P())
    return jax.shard_map(
        body, mesh=mesh, in_specs=placed, out_specs=P("rows", "cols"), check_vma=False
    )
```

time: 713 us -> 159 us (0.22); the launches traced: 704 us -> 159 us
  waiting for transfers between devices: 497 us -> 0 us
  Pallas kernels: 0 us -> 157 us
  matrix products: 97.6 us -> 0 us
  blocking collectives: 37.1 us -> 0 us
  starting transfers between devices: 22.4 us -> 0 us
  between operations: 17.1 us -> 0.01 us
  other arithmetic: 14.5 us -> 0 us
  local copies, waits for them, and re-layouts: 16 us -> 2.26 us
    psum x5 -> x0, waiting for transfers between devices: 409 us -> none  [body(): gram_sum = lax.psum(local_gram, 'rows')]
    pallas_call x0 -> x1, Pallas kernels: none -> 157 us  [body(): pl.pallas_call(kernel, out_shape=jax.ShapeDtypeStruct(matrix.shape, F32),...]
    dot_general x130 -> x0, matrix products: 97.6 us -> none  [the longest x60 35.9 us: advance(): return 1.5 * current - 0.5 * jnp.dot(current, inner, precision=highest)]
    ppermute x3 -> x0, waiting for transfers between devices: 58.3 us -> none  [from_behind(): lax.ppermute(array, axis, [(i, (i + by) % count) for i in range(count)])]
    all_to_all x2 -> x0, blocking collectives: 37.1 us -> none  [body(): lax.all_to_all(chosen, 'cols', split_axis=0, concat_axis=0, tiled=True)]
    all_to_all x2 -> x0, waiting for transfers between devices: 30.1 us -> none  [body(): lax.all_to_all(pieces, 'cols', split_axis=0, concat_axis=0, tiled=True)]
    gather x7 -> x0, local copies, waits for them, and re-layouts: 14.1 us -> none  [the longest x5 12.8 us: start_iterate(): scale = lax.rsqrt(jnp.diagonal(gram_full) + epsilon)]
    all_to_all x2 -> x0, starting transfers between devices: 12.7 us -> none  [body(): lax.all_to_all(pieces, 'cols', split_axis=0, concat_axis=0, tiled=True)]
  transfers between devices with their start and end apart: 10 -> 0, of which waited for: 10 -> 0; matrix products, arithmetic and copies ran while one was open for 0% -> 0% of each run, Pallas kernels for 0% -> 0%
where the time goes in v3:
time: 159 us
  Pallas kernels  157 us (99%)
  local copies, waits for them, and re-layouts  2.26 us (1%)
    pallas_call x1, Pallas kernels, body(): pl.pallas_call(kernel, out_shape=jax.ShapeDtypeStruct(matrix.shape, F32),...  157 us

profile of v3, /device:TPU:1, one launch (start us, length us, event | category | flops | bytes accessed | tf_op | source)
XLA Modules:
  0.0 159.2 jit_solution(14257283196404221923)
XLA Ops:
  0.0 156.9 %shard_map.28 = f32[2048,128]{1,0:T(8,128)} custom-call(s32[2,8]{1,0:T(2,128)} %table.1, f32[2048,128]{1,0:T(8,128)} %a.1), custom_call_target="tpu_custom_call" | custom-call | tf_op jit(solution)/shard_map/pallas_call | solution.py:322
  156.9 2.3 %copy.4 = f32[2048,128]{1,0:T(8,128)} copy(f32[2048,128]{1,0:T(8,128)} %shard_map.28) | data formatting | bytes 2097152

commit v4 on v3

v4 whole, which is shorter than its diff:
```python
import jax
import jax.numpy as jnp
from jax import lax
from jax.experimental import pallas as pl
from jax.experimental.pallas import tpu as pltpu
from jax.sharding import PartitionSpec as P

F32, BF = jnp.float32, jnp.bfloat16
MESH = pl.DeviceIdType.MESH
CYCLE = 3
STEPS = 12
EPS = 1e-6
W = 128
NB = 8
OWN = NB // 2
SIDE = 4
SLAB = 512
NEAR = 5
PART = OWN * W
LINE = PART // SIDE
UNIT = LINE // SIDE**2
ROWS = NEAR * PART
ORDERS = ((0, 1, 2), (1, 2, 0), (2, 0, 1), (0, 1, 2), (1, 2, 0))
FIRST, REST = (0, 1), (2, 3, 4)


def split(x):
    high = x.astype(BF)
    return high, (x - high.astype(F32)).astype(BF)


def dot(a, b):
    return jnp.dot(a, b, preferred_element_type=F32)


def dot_nt(a, b):
    return lax.dot_general(a, b, (((1,), (1,)), ((), ())), preferred_element_type=F32)


def dot3(a, b):
    (ah, al), (bh, bl) = a, b
    return dot(jnp.concatenate([ah, ah, al], 1), jnp.concatenate([bh, bl, bh], 0))


def start(aa, ab, ba, bb):
    g = jnp.concatenate([jnp.concatenate([aa, ab], 1), jnp.concatenate([ba, bb], 1)], 0)
    r = lax.broadcasted_iota(jnp.int32, g.shape, 0)
    c = lax.broadcasted_iota(jnp.int32, g.shape, 1)
    diagonal = jnp.where(r == c, g, 0.0)
    tall = lax.rsqrt(jnp.sum(diagonal, axis=1, keepdims=True) + EPS)
    wide = lax.rsqrt(jnp.sum(diagonal, axis=0, keepdims=True) + EPS)
    normed = g * tall * wide
    k = jnp.where(r < c, normed, jnp.where(r > c, -normed, 1.0))
    total = jnp.sum(jnp.sum(k * k, axis=1, keepdims=True), axis=0, keepdims=True)
    return k / jnp.sqrt(total)


def polar_steps(x, count, problems=OWN):
    def step(_, carry):
        now = [x[n] for n in range(problems)]
        halves = [split(v) for v in now]
        crossed = [dot_nt(h, l) for h, l in halves]
        plain = [dot_nt(h, h) for h, _ in halves]
        inner = [split(p + (c + c.T)) for p, c in zip(plain, crossed)]
        outer = [dot3(i, h) for i, h in zip(inner, halves)]
        for n in range(problems):
            x[n] = 1.5 * now[n] - 0.5 * outer[n]
        return carry

    lax.fori_loop(0, count, step, 0, unroll=2)


def place():
    r, k = lax.axis_index("rows"), lax.axis_index("cols")
    return (lax.rem(r, SIDE), r // SIDE, k // 2), lax.rem(k, 2), k


def device(at, core):
    return (at[1] * SIDE + at[0], at[2] * 2 + core)


def moved(at, axis, by):
    new = list(at)
    new[axis] = lax.rem(at[axis] + by, SIDE)
    return tuple(new)


def greet(peers):
    barrier = pltpu.get_barrier_semaphore()
    for peer in peers:
        pl.semaphore_signal(barrier, inc=1, device_id=peer, device_id_type=MESH)
    pl.semaphore_wait(barrier, len(peers))


def remote(src, dst, send, recv, to):
    return pltpu.make_async_remote_copy(
        src_ref=src, dst_ref=dst, send_sem=send, recv_sem=recv, device_id=to, device_id_type=MESH
    )


def rows_at(start, size, unit):
    return pl.ds(pl.multiple_of(start, unit), size)


def partner(table, meeting, j):
    if meeting < CYCLE:
        return (j + NB - meeting - 1) % NB if isinstance(j, int) else lax.rem(j + NB - meeting - 1, NB)
    return table[meeting - CYCLE, j]


def column(g, j, count=NB):
    return jnp.concatenate([g[j * count + i] for i in range(count)], 0)


def beside(g, other, j, count=NB):
    return split(jnp.concatenate([column(g, other, count), column(g, j, count)], 1))


def kernel(table, a, out, wide, high, low, high_t, low_t, part, land, small, gs, g0, g1, g2, g3, x, q, ql, th, tl, w2, w3, w4,
           a_send, a_recv, f_send, f_recv, r_send, r_recv, u_send, u_recv, v_send, v_recv, s_send, s_recv, c_send, c_recv,
           q_send, q_recv, g_send, g_recv, w_send, w_recv, d_send, d_recv):
    at, core, k = place()
    z = at[2]
    sibling = device(at, 1 - core)
    near = [
        (dx, dy, dz) for dx in range(SIDE) for dy in range(SIDE) for dz in range(SIDE)
        if 0 in (dx, dy, dz) and (dx or dy or dz)
    ]
    greet([sibling] + [device(moved(moved(moved(at, 0, dx), 1, dy), 2, dz), core) for dx, dy, dz in near])
    pending = []

    def go(copy):
        copy.start()
        pending.append(copy)
        return copy

    def arrive(copies):
        for copy in copies:
            copy.wait_recv()

    def slab(where):
        return rows_at(where * SLAB, SLAB, SLAB)

    arrivals = []
    for by in (1, 2, 3):
        to = moved(at, 2, by)
        arrivals.append(go(remote(
            a.at[slab(to[2])], wide.at[k, slab(to[2])], a_send.at[by - 1], a_recv.at[by - 1], device(to, core)
        )))
    own = slab(z)
    across = [go(remote(a.at[own], wide.at[k, own], f_send.at[0], f_recv.at[0], sibling))]

    def settle(block, value):
        h, l = split(value)
        high[block] = h
        low[block] = l
        high_t[block] = h.T
        low_t[block] = l.T

    settle(k, a[own, :])
    wide[k] = a[...]
    for by in (1, 2, 3):
        block = lax.rem(z + SIDE - by, SIDE) * 2 + core
        arrivals[by - 1].wait_recv()
        across.append(go(remote(
            wide.at[block, own], wide.at[block, own], f_send.at[by], f_recv.at[by], sibling
        )))
        settle(block, wide[block, own, :])
    for by in range(4):
        block = lax.rem(z + SIDE - by, SIDE) * 2 + 1 - core
        across[by].wait_recv()
        settle(block, wide[block, own, :])

    for t in range(OWN):
        j = 2 * t + core
        ids = [lax.rem(j - d + NB, NB) for d in range(NEAR)]
        left = jnp.concatenate([jnp.concatenate([high_t[i], high_t[i], low_t[i]], 1) for i in ids], 0)
        column_sum = dot(left, jnp.concatenate([high[j], low[j], high[j]], 0))
        for d in range(NEAR):
            part[d * PART + t * W:d * PART + (t + 1) * W, :] = column_sum[d * W:(d + 1) * W]

    def line(p):
        axis = ORDERS[p][0]
        return [(by, moved(at, axis, by)) for by in (1, 2, 3)]

    def plane(p):
        _, one, two = ORDERS[p]
        return [
            (u * SIDE + v, moved(moved(at, one, u), two, v)) for u in range(SIDE) for v in range(SIDE) if u or v
        ]

    def strip(p, where):
        return p * PART + where[ORDERS[p][0]] * LINE

    def grain(p, where):
        _, one, two = ORDERS[p]
        return strip(p, at) + (where[one] * SIDE + where[two]) * UNIT

    waiting = [
        [
            go(remote(
                part.at[rows_at(strip(p, to), LINE, 8)], land.at[p, by - 1],
                r_send.at[p, by - 1], r_recv.at[p, by - 1], device(to, core),
            ))
            for by, to in line(p)
        ]
        for p in range(NEAR)
    ]
    for p in range(NEAR):
        arrive(waiting[p])
        mine = rows_at(strip(p, at), LINE, 8)
        part[mine, :] = part[mine, :] + land[p, 0] + land[p, 1] + land[p, 2]
        waiting[p] = [
            go(remote(
                part.at[rows_at(grain(p, to), UNIT, 8)], small.at[p, by - 1],
                u_send.at[p, by - 1], u_recv.at[p, by - 1], device(to, core),
            ))
            for by, to in plane(p)
        ]
    for p in range(NEAR):
        arrive(waiting[p])
        mine = rows_at(grain(p, at), UNIT, 8)
        total = part[mine, :]
        for by in range(SIDE * SIDE - 1):
            total = total + small[p, by]
        gs[core, mine, :] = total
        done = gs.at[core, mine]
        waiting[p] = [
            go(remote(done, done, v_send.at[p, by - 1], v_recv.at[p, by - 1], device(to, core)))
            for by, to in plane(p)
        ]

    def widen(p):
        arrive(waiting[p])
        done = gs.at[core, rows_at(strip(p, at), LINE, 8)]
        waiting[p] = [
            go(remote(done, done, s_send.at[p, by - 1], s_recv.at[p, by - 1], device(to, core)))
            for by, to in line(p)
        ]

    def cross(p):
        arrive(waiting[p])
        done = gs.at[core, pl.ds(p * PART, PART)]
        waiting[p] = [go(remote(done, done, c_send.at[p], c_recv.at[p], sibling))]

    for p in FIRST:
        widen(p)
    for p in FIRST:
        cross(p)
    for p in FIRST:
        arrive(waiting[p])

    def summed(j, d):
        return gs[lax.rem(j, 2), rows_at(d * PART + (j // 2) * W, W, W), :]

    grams = (g0, g1, g2)
    mine = [2 * n + core for n in range(OWN)]
    for n, j in enumerate(mine):
        before = partner(table, 0, j)
        ab = summed(j, 1)
        x[n] = start(summed(before, 0), ab, ab.T, summed(j, 0))
    polar_steps(x, 4)
    for p in REST:
        widen(p)
    polar_steps(x, 4)
    for p in REST:
        cross(p)
    polar_steps(x, 4)
    for p in REST:
        arrive(waiting[p])
    for j in range(NB):
        for i in range(NB):
            d = (j - i) % NB
            c, e, f = (j, d, j // 2) if d < NEAR else (i, NB - d, i // 2)
            block = gs[c % 2, e * PART + f * W:e * PART + (f + 1) * W, :]
            g0[j * NB + i] = block if d < NEAR else block.T

    coming = {}
    for by in (1, 2, 3):
        to = moved(at, 2, by)
        for more in (1, 2, 3):
            rest = slab(lax.rem(to[2] + more, SIDE))
            coming[by, more] = go(remote(
                a.at[rest], wide.at[k, rest], w_send.at[by - 1, more - 1], w_recv.at[by - 1, more - 1], device(to, core)
            ))

    for m in (0, 1):
        g, after = grams[m], grams[m + 1]
        if m:
            for n, j in enumerate(mine):
                other = partner(table, m, j)
                x[n] = start(g[other * NB + other], g[j * NB + other], g[other * NB + j], g[j * NB + j])
            polar_steps(x, STEPS)
        q[m, core] = x[:, :, W:]
        swap = go(remote(q.at[m, core], q.at[m, core], q_send.at[m], q_recv.at[m], sibling))
        for n, j in enumerate(mine):
            h, l = split(dot3(beside(g, partner(table, m, j), j), split(q[m, core, n])))
            th[n * NB:(n + 1) * NB] = h.reshape(NB, W, W)
            tl[n * NB:(n + 1) * NB] = l.reshape(NB, W, W)
        swap.wait_recv()
        turned = [split(q[m, i % 2, i // 2].T) for i in range(NB)]
        arriving = []
        for two in (0, 2):
            made = []
            for i in range(NB):
                other = partner(table, m, i)
                right = tuple(
                    jnp.concatenate([
                        jnp.concatenate([s[n * NB + other], s[n * NB + i]], 0) for n in (two, two + 1)
                    ], 1)
                    for s in (th, tl)
                )
                made.append(dot3(turned[i], right))
            for e, n in enumerate((two, two + 1)):
                for i in range(NB):
                    after[mine[n] * NB + i] = made[i][:, e * W:(e + 1) * W]
                done = after.at[pl.ds(mine[n] * NB, NB)]
                arriving.append(go(remote(done, done, g_send.at[m, n], g_recv.at[m, n], sibling)))
        if m:
            for j in range(NB):
                far = (j - 2) % NB
                old = [split(q[0, i % 2, i // 2]) for i in (far, j)]
                new = split(q[1, j % 2, j // 2])
                pieces = [
                    dot3(old[0], tuple(v[:W] for v in new)), dot3(old[1], tuple(v[W:] for v in new))
                ]
                for i in range(NB):
                    w2[j * NB + i] = jnp.zeros((W, W), F32)
                for e, i in enumerate(((j - 3) % NB, (j - 2) % NB, (j - 1) % NB, j)):
                    w2[j * NB + i] = pieces[e // 2][(e % 2) * W:(e % 2 + 1) * W]
        arrive(arriving)

    last = table[1, k]
    ids = [k, table[0, k], last, table[0, last]]
    others = [partner(table, 2, j) for j in ids]
    for n, (j, other) in enumerate(zip(ids, others)):
        x[n] = start(g2[other * NB + other], g2[j * NB + other], g2[other * NB + j], g2[j * NB + j])
    polar_steps(x, STEPS)
    ql[...] = x[:, :, W:]
    for n, (j, other) in enumerate(zip(ids, others)):
        factor = split(ql[n])
        h, l = split(dot3(beside(g2, other, j), factor))
        th[n * NB:(n + 1) * NB] = h.reshape(NB, W, W)
        tl[n * NB:(n + 1) * NB] = l.reshape(NB, W, W)
        w3[n * NB:(n + 1) * NB] = dot3(beside(w2, other, j), factor).reshape(NB, W, W)
    for e in range(OWN):
        right = tuple(
            jnp.concatenate([
                jnp.concatenate([s[n * NB + others[e]], s[n * NB + ids[e]]], 0) for n in range(OWN)
            ], 1)
            for s in (th, tl)
        )
        made = dot3(split(ql[e].T), right)
        for n in range(OWN):
            g3[n * OWN + e] = made[:, n * W:(n + 1) * W]

    passing = []
    for more in (1, 2, 3):
        rest = slab(lax.rem(z + more, SIDE))
        for by in range(4):
            block = lax.rem(z + SIDE - by, SIDE) * 2 + core
            if by:
                coming[by, more].wait_recv()
            passing.append(go(remote(
                wide.at[block, rest], wide.at[block, rest], d_send.at[by, more - 1], d_recv.at[by, more - 1], sibling
            )))

    pairs = ((1, 0), (3, 2))
    for n, (other, j) in enumerate(pairs):
        x[n] = start(g3[other * OWN + other], g3[j * OWN + other], g3[other * OWN + j], g3[j * OWN + j])
    polar_steps(x, STEPS, 2)
    factors = [x[n, :, W:] for n in range(2)]
    halves = [split(f) for f in factors]
    tall = [dot3(beside(g3, other, j, OWN), h) for (other, j), h in zip(pairs, halves)]
    corners = [
        [
            dot3(split(factors[e].T), split(jnp.concatenate([
                tall[n][other * W:(other + 1) * W], tall[n][j * W:(j + 1) * W]
            ], 0)))
            for n in range(2)
        ]
        for e, (other, j) in enumerate(pairs)
    ]
    for n, (other, j) in enumerate(pairs):
        w4[n * NB:(n + 1) * NB] = dot3(beside(w3, other, j), halves[n]).reshape(NB, W, W)
    x[0] = start(corners[1][1], corners[1][0], corners[0][1], corners[0][0])
    polar_steps(x, STEPS, 1)
    wh, wl = split(dot3(beside(w4, 1, 0), split(x[0, :, W:])))
    w_right = jnp.concatenate([wh, wl, wh], 0)
    arrive(passing)

    def rotate(turn, carry):
        tile = rows_at(turn * SLAB, SLAB, SLAB)
        lh, ll = split(jnp.concatenate([wide[i, tile, :] for i in range(NB)], 1))
        out[tile, :] = dot(jnp.concatenate([lh, lh, ll], 1), w_right)
        return carry

    lax.fori_loop(0, SIDE, rotate, 0)
    for copy in pending:
        copy.wait_send()


def body(matrix, partners):
    vmem = pl.BlockSpec(memory_space=pltpu.VMEM)
    dma = pltpu.SemaphoreType.DMA
    square = (NB * NB, W, W)
    quarter = (OWN * NB, W, W)
    return pl.pallas_call(
        kernel,
        out_shape=jax.ShapeDtypeStruct(matrix.shape, F32),
        in_specs=[pl.BlockSpec(memory_space=pltpu.SMEM), vmem],
        out_specs=vmem,
        scratch_shapes=[
            pltpu.VMEM((NB, SIDE * SLAB, W), F32),
            pltpu.VMEM((NB, SLAB, W), BF),
            pltpu.VMEM((NB, SLAB, W), BF),
            pltpu.VMEM((NB, W, SLAB), BF),
            pltpu.VMEM((NB, W, SLAB), BF),
            pltpu.VMEM((ROWS, W), F32),
            pltpu.VMEM((NEAR, 3, LINE, W), F32),
            pltpu.VMEM((NEAR, SIDE**2 - 1, UNIT, W), F32),
            pltpu.VMEM((2, ROWS, W), F32),
        ] + [pltpu.VMEM(square, F32)] * 3 + [
            pltpu.VMEM((OWN * OWN, W, W), F32),
            pltpu.VMEM((OWN, 2 * W, 2 * W), F32),
            pltpu.VMEM((2, 2, OWN, 2 * W, W), F32),
            pltpu.VMEM((OWN, 2 * W, W), F32),
            pltpu.VMEM(quarter, BF),
            pltpu.VMEM(quarter, BF),
            pltpu.VMEM(square, F32),
            pltpu.VMEM(quarter, F32),
            pltpu.VMEM((2 * NB, W, W), F32),
            dma((3,)), dma((3,)), dma((4,)), dma((4,)),
            dma((NEAR, 3)), dma((NEAR, 3)), dma((NEAR, 15)), dma((NEAR, 15)), dma((NEAR, 15)), dma((NEAR, 15)),
            dma((NEAR, 3)), dma((NEAR, 3)), dma((NEAR,)), dma((NEAR,)),
            dma((2,)), dma((2,)), dma((2, OWN)), dma((2, OWN)), dma((3, 3)), dma((3, 3)), dma((4, 3)), dma((4, 3)),
        ],
        compiler_params=pltpu.CompilerParams(
            collective_id=0, has_side_effects=True, vmem_limit_bytes=54 * 2**20
        ),
    )(partners, matrix)


def solution(mesh):
    placed = (P("rows", "cols"), P())
    return jax.shard_map(
        body, mesh=mesh, in_specs=placed, out_specs=P("rows", "cols"), check_vma=False
    )
```

time: 159 us -> 132 us (0.83)
  Pallas kernels: 157 us -> 129 us
    pallas_call x1, Pallas kernels: 157 us -> 129 us  [body(): pl.pallas_call(kernel, out_shape=jax.ShapeDtypeStruct(matrix.shape, F32),...]
where the time goes in v4:
time: 132 us
  Pallas kernels  129 us (98%)
  local copies, waits for them, and re-layouts  2.26 us (2%)
    pallas_call x1, Pallas kernels, body(): pl.pallas_call(kernel, out_shape=jax.ShapeDtypeStruct(matrix.shape, F32),...  129 us

profile of v4, /device:TPU:1, one launch (start us, length us, event | category | flops | bytes accessed | tf_op | source)
XLA Modules:
  0.0 131.8 jit_solution(16116807009016792582)
XLA Ops:
  0.0 129.5 %shard_map.28 = f32[2048,128]{1,0:T(8,128)} custom-call(s32[2,8]{1,0:T(2,128)} %table.1, f32[2048,128]{1,0:T(8,128)} %a.1), custom_call_target="tpu_custom_call" | custom-call | tf_op jit(solution)/shard_map/pallas_call | solution.py:408
  129.5 2.3 %copy.4 = f32[2048,128]{1,0:T(8,128)} copy(f32[2048,128]{1,0:T(8,128)} %shard_map.28) | data formatting | bytes 2097152

commit v5 on v4

--- a/solution.py
+++ b/solution.py
@@ -9,6 +9,7 @@
 MESH = pl.DeviceIdType.MESH
 CYCLE = 3
 STEPS = 12
+TURNS = 4
 EPS = 1e-6
 W = 128
 NB = 8
@@ -55,19 +56,34 @@
     return k / jnp.sqrt(total)
 
 
+def polar_step(x, problems):
+    now = [x[n] for n in range(problems)]
+    halves = [split(v) for v in now]
+    crossed = [dot_nt(h, l) for h, l in halves]
+    plain = [dot_nt(h, h) for h, _ in halves]
+    inner = [split(p + (c + c.T)) for p, c in zip(plain, crossed)]
+    outer = [dot3(i, h) for i, h in zip(inner, halves)]
+    for n in range(problems):
+        x[n] = 1.5 * now[n] - 0.5 * outer[n]
+
+
 def polar_steps(x, count, problems=OWN):
     def step(_, carry):
-        now = [x[n] for n in range(problems)]
-        halves = [split(v) for v in now]
-        crossed = [dot_nt(h, l) for h, l in halves]
-        plain = [dot_nt(h, h) for h, _ in halves]
-        inner = [split(p + (c + c.T)) for p, c in zip(plain, crossed)]
-        outer = [dot3(i, h) for i, h in zip(inner, halves)]
-        for n in range(problems):
-            x[n] = 1.5 * now[n] - 0.5 * outer[n]
+        polar_step(x, problems)
         return carry
 
     lax.fori_loop(0, count, step, 0, unroll=2)
+
+
+def polar_beside(x, problems, work):
+    def turn(t, carry):
+        polar_step(x, problems)
+        work(t)
+        for _ in range(STEPS // TURNS - 1):
+            polar_step(x, problems)
+        return carry
+
+    lax.fori_loop(0, TURNS, turn, 0)
 
 
 def place():
@@ -116,7 +132,7 @@
     return split(jnp.concatenate([column(g, other, count), column(g, j, count)], 1))
 
 
-def kernel(table, a, out, wide, high, low, high_t, low_t, part, land, small, gs, g0, g1, g2, g3, x, q, ql, th, tl, w2, w3, w4,
+def kernel(table, a, out, wide, high, low, high_t, low_t, part, land, small, gs, g0, g1, g2, g3, x, q, ql, th, tl, w3, w4, paired,
            a_send, a_recv, f_send, f_recv, r_send, r_recv, u_send, u_recv, v_send, v_recv, s_send, s_recv, c_send, c_recv,
            q_send, q_recv, g_send, g_recv, w_send, w_recv, d_send, d_recv):
     at, core, k = place()
@@ -247,8 +263,7 @@
         widen(p)
     for p in FIRST:
         cross(p)
-    for p in FIRST:
-        arrive(waiting[p])
+    arrive(waiting[0])
 
     def summed(j, d):
         return gs[lax.rem(j, 2), rows_at(d * PART + (j // 2) * W, W, W), :]
@@ -266,7 +281,7 @@
     for p in REST:
         cross(p)
     polar_steps(x, 4)
-    for p in REST:
+    for p in (1,) + REST:
         arrive(waiting[p])
     for j in range(NB):
         for i in range(NB):
@@ -284,6 +299,7 @@
                 a.at[rest], wide.at[k, rest], w_send.at[by - 1, more - 1], w_recv.at[by - 1, more - 1], device(to, core)
             ))
 
+    w2 = g0
     for m in (0, 1):
         g, after = grams[m], grams[m + 1]
         if m:
@@ -291,6 +307,7 @@
                 other = partner(table, m, j)
                 x[n] = start(g[other * NB + other], g[j * NB + other], g[other * NB + j], g[j * NB + j])
             polar_steps(x, STEPS)
+            arrive(arriving)
         q[m, core] = x[:, :, W:]
         swap = go(remote(q.at[m, core], q.at[m, core], q_send.at[m], q_recv.at[m], sibling))
         for n, j in enumerate(mine):
@@ -328,7 +345,7 @@
                     w2[j * NB + i] = jnp.zeros((W, W), F32)
                 for e, i in enumerate(((j - 3) % NB, (j - 2) % NB, (j - 1) % NB, j)):
                     w2[j * NB + i] = pieces[e // 2][(e % 2) * W:(e % 2 + 1) * W]
-        arrive(arriving)
+    arrive(arriving)
 
     last = table[1, k]
     ids = [k, table[0, k], last, table[0, last]]
@@ -338,11 +355,9 @@
     polar_steps(x, STEPS)
     ql[...] = x[:, :, W:]
     for n, (j, other) in enumerate(zip(ids, others)):
-        factor = split(ql[n])
-        h, l = split(dot3(beside(g2, other, j), factor))
+        h, l = split(dot3(beside(g2, other, j), split(ql[n])))
         th[n * NB:(n + 1) * NB] = h.reshape(NB, W, W)
         tl[n * NB:(n + 1) * NB] = l.reshape(NB, W, W)
-        w3[n * NB:(n + 1) * NB] = dot3(beside(w2, other, j), factor).reshape(NB, W, W)
     for e in range(OWN):
         right = tuple(
             jnp.concatenate([
@@ -368,7 +383,14 @@
     pairs = ((1, 0), (3, 2))
     for n, (other, j) in enumerate(pairs):
         x[n] = start(g3[other * OWN + other], g3[j * OWN + other], g3[other * OWN + j], g3[j * OWN + j])
-    polar_steps(x, STEPS, 2)
+
+    def follow(t):
+        j = k + (t // 2) * (last - k)
+        j = j + lax.rem(t, 2) * (table[0, j] - j)
+        new = dot3(beside(w2, partner(table, 2, j), j), split(ql[t]))
+        w3[pl.ds(t * NB, NB)] = new.reshape(NB, W, W)
+
+    polar_beside(x, 2, follow)
     factors = [x[n, :, W:] for n in range(2)]
     halves = [split(f) for f in factors]
     tall = [dot3(beside(g3, other, j, OWN), h) for (other, j), h in zip(pairs, halves)]
@@ -384,15 +406,21 @@
     for n, (other, j) in enumerate(pairs):
         w4[n * NB:(n + 1) * NB] = dot3(beside(w3, other, j), halves[n]).reshape(NB, W, W)
     x[0] = start(corners[1][1], corners[1][0], corners[0][1], corners[0][0])
-    polar_steps(x, STEPS, 1)
-    wh, wl = split(dot3(beside(w4, 1, 0), split(x[0, :, W:])))
+    wh, wl = beside(w4, 1, 0)
     w_right = jnp.concatenate([wh, wl, wh], 0)
     arrive(passing)
 
-    def rotate(turn, carry):
-        tile = rows_at(turn * SLAB, SLAB, SLAB)
+    def follow_rows(t):
+        tile = slab(t)
         lh, ll = split(jnp.concatenate([wide[i, tile, :] for i in range(NB)], 1))
-        out[tile, :] = dot(jnp.concatenate([lh, lh, ll], 1), w_right)
+        paired[tile, :] = dot(jnp.concatenate([lh, lh, ll], 1), w_right)
+
+    polar_beside(x, 1, follow_rows)
+    factor = split(x[0, :, W:])
+
+    def rotate(t, carry):
+        tile = slab(t)
+        out[tile, :] = dot3(split(paired[tile, :]), factor)
         return carry
 
     lax.fori_loop(0, SIDE, rotate, 0)
@@ -427,16 +455,16 @@
             pltpu.VMEM((OWN, 2 * W, W), F32),
             pltpu.VMEM(quarter, BF),
             pltpu.VMEM(quarter, BF),
-            pltpu.VMEM(square, F32),
             pltpu.VMEM(quarter, F32),
             pltpu.VMEM((2 * NB, W, W), F32),
+            pltpu.VMEM((SIDE * SLAB, 2 * W), F32),
             dma((3,)), dma((3,)), dma((4,)), dma((4,)),
             dma((NEAR, 3)), dma((NEAR, 3)), dma((NEAR, 15)), dma((NEAR, 15)), dma((NEAR, 15)), dma((NEAR, 15)),
             dma((NEAR, 3)), dma((NEAR, 3)), dma((NEAR,)), dma((NEAR,)),
             dma((2,)), dma((2,)), dma((2, OWN)), dma((2, OWN)), dma((3, 3)), dma((3, 3)), dma((4, 3)), dma((4, 3)),
         ],
         compiler_params=pltpu.CompilerParams(
-            collective_id=0, has_side_effects=True, vmem_limit_bytes=54 * 2**20
+            collective_id=0, has_side_effects=True, vmem_limit_bytes=46 * 2**20
         ),
     )(partners, matrix)
 

time: 132 us -> 125 us (0.947)
  Pallas kernels: 129 us -> 122 us
    pallas_call x1, Pallas kernels: 129 us -> 122 us  [body(): pl.pallas_call(kernel, out_shape=jax.ShapeDtypeStruct(matrix.shape, F32),...]
    unnamed x1 -> x5, local copies, waits for them, and re-layouts: 2.26 us -> 2.88 us
where the time goes in v5:
time: 125 us
  Pallas kernels  122 us (98%)
  local copies, waits for them, and re-layouts  2.88 us (2%)
    pallas_call x1, Pallas kernels, body(): pl.pallas_call(kernel, out_shape=jax.ShapeDtypeStruct(matrix.shape, F32),...  122 us
    unnamed x5, local copies, waits for them, and re-layouts  2.88 us

profile of v5, /device:TPU:1, one launch (start us, length us, event | category | flops | bytes accessed | tf_op | source)
XLA Modules:
  0.0 125.2 jit_solution(11913332744602494038)
XLA Ops:
  0.0 0.0 copy-start
  0.0 1.2 copy-done
  1.2 0.0 copy-start.1
  1.2 0.7 copy-done.1
  1.9 122.3 %shard_map.28 = f32[2048,128]{1,0:T(8,128)S(1)} custom-call(s32[2,8]{1,0:T(2,128)S(1)} %copy-done.1, f32[2048,128]{1,0:T(8,128)S(1)} %copy-done), custom_call_target="tpu_custom_call" | custom-call | tf_op jit(solution)/shard_map/pallas_call | solution.py:436
  124.2 1.0 copy.4
Async XLA Ops:
  0.0 1.2 copy-start
  1.2 0.7 copy-start.1

commit v6 on v5

--- a/solution.py
+++ b/solution.py
@@ -138,11 +138,7 @@
     at, core, k = place()
     z = at[2]
     sibling = device(at, 1 - core)
-    near = [
-        (dx, dy, dz) for dx in range(SIDE) for dy in range(SIDE) for dz in range(SIDE)
-        if 0 in (dx, dy, dz) and (dx or dy or dz)
-    ]
-    greet([sibling] + [device(moved(moved(moved(at, 0, dx), 1, dy), 2, dz), core) for dx, dy, dz in near])
+    greet([sibling] + [device(moved(at, axis, by), core) for axis in range(3) for by in (1, 2, 3)])
     pending = []
 
     def go(copy):
@@ -277,6 +273,16 @@
     polar_steps(x, 4)
     for p in REST:
         widen(p)
+
+    coming = {}
+    for by in (1, 2, 3):
+        to = moved(at, 2, by)
+        for more in (1, 2, 3):
+            rest = slab(lax.rem(to[2] + more, SIDE))
+            coming[by, more] = go(remote(
+                a.at[rest], wide.at[k, rest], w_send.at[by - 1, more - 1], w_recv.at[by - 1, more - 1], device(to, core)
+            ))
+
     polar_steps(x, 4)
     for p in REST:
         cross(p)
@@ -289,15 +295,6 @@
             c, e, f = (j, d, j // 2) if d < NEAR else (i, NB - d, i // 2)
             block = gs[c % 2, e * PART + f * W:e * PART + (f + 1) * W, :]
             g0[j * NB + i] = block if d < NEAR else block.T
-
-    coming = {}
-    for by in (1, 2, 3):
-        to = moved(at, 2, by)
-        for more in (1, 2, 3):
-            rest = slab(lax.rem(to[2] + more, SIDE))
-            coming[by, more] = go(remote(
-                a.at[rest], wide.at[k, rest], w_send.at[by - 1, more - 1], w_recv.at[by - 1, more - 1], device(to, core)
-            ))
 
     w2 = g0
     for m in (0, 1):

time: 125 us -> 134 us (1.072)
  the two profiles are of different devices: /device:TPU:1 before, /device:TPU:97 now
where the time goes in v6:
time: 134 us
  Pallas kernels  131 us (98%)
  local copies, waits for them, and re-layouts  2.88 us (2%)
    pallas_call x1, Pallas kernels, body(): pl.pallas_call(kernel, out_shape=jax.ShapeDtypeStruct(matrix.shape, F32),...  131 us
    unnamed x5, local copies, waits for them, and re-layouts  2.88 us

profile of v6, /device:TPU:97, one launch (start us, length us, event | category | flops | bytes accessed | tf_op | source)
XLA Modules:
  0.0 134.0 jit_solution(12525675367098001965)
XLA Ops:
  0.0 0.0 copy-start
  0.0 1.2 copy-done
  1.2 0.0 copy-start.1
  1.2 0.7 copy-done.1
  1.9 131.2 %shard_map.28 = f32[2048,128]{1,0:T(8,128)S(1)} custom-call(s32[2,8]{1,0:T(2,128)S(1)} %copy-done.1, f32[2048,128]{1,0:T(8,128)S(1)} %copy-done), custom_call_target="tpu_custom_call" | custom-call | tf_op jit(solution)/shard_map/pallas_call | solution.py:433
  133.1 1.0 copy.4
Async XLA Ops:
  0.0 1.2 copy-start
  1.2 0.7 copy-start.1

commit v7 on v5

--- a/solution.py
+++ b/solution.py
@@ -44,16 +44,22 @@
 
 
 def start(aa, ab, ba, bb):
-    g = jnp.concatenate([jnp.concatenate([aa, ab], 1), jnp.concatenate([ba, bb], 1)], 0)
-    r = lax.broadcasted_iota(jnp.int32, g.shape, 0)
-    c = lax.broadcasted_iota(jnp.int32, g.shape, 1)
-    diagonal = jnp.where(r == c, g, 0.0)
-    tall = lax.rsqrt(jnp.sum(diagonal, axis=1, keepdims=True) + EPS)
-    wide = lax.rsqrt(jnp.sum(diagonal, axis=0, keepdims=True) + EPS)
-    normed = g * tall * wide
-    k = jnp.where(r < c, normed, jnp.where(r > c, -normed, 1.0))
-    total = jnp.sum(jnp.sum(k * k, axis=1, keepdims=True), axis=0, keepdims=True)
-    return k / jnp.sqrt(total)
+    r = lax.broadcasted_iota(jnp.int32, aa.shape, 0)
+    c = lax.broadcasted_iota(jnp.int32, aa.shape, 1)
+    diagonals = [jnp.where(r == c, v, 0.0) for v in (aa, bb)]
+    tall = [lax.rsqrt(jnp.sum(v, axis=1, keepdims=True) + EPS) for v in diagonals]
+    wide = [lax.rsqrt(jnp.sum(v, axis=0, keepdims=True) + EPS) for v in diagonals]
+
+    def skewed(v, e):
+        normed = v * tall[e] * wide[e]
+        return jnp.where(r < c, normed, jnp.where(r > c, -normed, 1.0))
+
+    k = jnp.concatenate([
+        jnp.concatenate([skewed(aa, 0), ab * tall[0] * wide[1]], 1),
+        jnp.concatenate([-(ba * tall[1] * wide[0]), skewed(bb, 1)], 1),
+    ], 0)
+    total = jnp.sum(jnp.sum(k * k, axis=0, keepdims=True), axis=1, keepdims=True)
+    return k * (1.0 / jnp.sqrt(total))
 
 
 def polar_step(x, problems):
@@ -138,11 +144,7 @@
     at, core, k = place()
     z = at[2]
     sibling = device(at, 1 - core)
-    near = [
-        (dx, dy, dz) for dx in range(SIDE) for dy in range(SIDE) for dz in range(SIDE)
-        if 0 in (dx, dy, dz) and (dx or dy or dz)
-    ]
-    greet([sibling] + [device(moved(moved(moved(at, 0, dx), 1, dy), 2, dz), core) for dx, dy, dz in near])
+    greet([sibling] + [device(moved(at, axis, by), core) for axis in range(3) for by in (1, 2, 3)])
     pending = []
 
     def go(copy):

time: 125 us -> 124 us (level)
  Pallas kernels: 122 us -> 120 us
    pallas_call x1, Pallas kernels: 122 us -> 120 us  [body(): pl.pallas_call(kernel, out_shape=jax.ShapeDtypeStruct(matrix.shape, F32),...]
where the time goes in v7:
time: 124 us; the launch traced here: 123 us
  Pallas kernels  120 us (97%)
  local copies, waits for them, and re-layouts  2.88 us (2%)
    pallas_call x1, Pallas kernels, body(): pl.pallas_call(kernel, out_shape=jax.ShapeDtypeStruct(matrix.shape, F32),...  120 us
    unnamed x5, local copies, waits for them, and re-layouts  2.88 us

profile of v7, /device:TPU:1, one launch (start us, length us, event | category | flops | bytes accessed | tf_op | source)
XLA Modules:
  0.0 123.3 jit_solution(14115666667646822469)
XLA Ops:
  0.0 0.0 copy-start
  0.0 1.2 copy-done
  1.2 0.0 copy-start.1
  1.2 0.7 copy-done.1
  1.9 120.5 %shard_map.28 = f32[2048,128]{1,0:T(8,128)S(1)} custom-call(s32[2,8]{1,0:T(2,128)S(1)} %copy-done.1, f32[2048,128]{1,0:T(8,128)S(1)} %copy-done), custom_call_target="tpu_custom_call" | custom-call | tf_op jit(solution)/shard_map/pallas_call | solution.py:438
  122.4 1.0 copy.4
Async XLA Ops:
  0.0 1.2 copy-start
  1.2 0.7 copy-start.1
